TPU v7x, 512 devices: a whole 4x8x8 slice. The times are simulated.
512 devices in a mesh: inst: 64 (over y, z), tp: 8 (over x, core).
Axes of the slice: x: 4, y: 8, z: 8, core: 2. Of those that a mesh axis runs over, the one named last changes fastest.
Arguments:
- queries: bfloat16 [256, 128, 128], P('inst', 'tp'), may hold values from -18 to 18
- new_keys: bfloat16 [256, 8, 128], P('inst', 'tp'), may hold values from -18 to 18
- new_values: bfloat16 [256, 8, 128], P('inst', 'tp'), may hold values from -6 to 6
- home_keys: bfloat16 [256, 256, 8, 128], P('inst', None, 'tp'), may hold values from -18 to 18
- home_values: bfloat16 [256, 256, 8, 128], P('inst', None, 'tp'), may hold values from -6 to 6
- home_len: int32 [256], P('inst'), may hold values from 1 to 256
- lent_keys: bfloat16 [4032, 32, 8, 128], P('inst', None, 'tp'), may hold values from -18 to 18
- lent_values: bfloat16 [4032, 32, 8, 128], P('inst', None, 'tp'), may hold values from -6 to 6
- lent_req: int32 [4032], replicated, may hold values from 0 to 255, as said below
- lent_len: int32 [4032], P('inst'), may hold values from 1 to 32
- out_weight: bfloat16 [16384, 16384], P('tp', 'inst'), may hold values from -0.046875 to 0.046875
- residual: bfloat16 [256, 16384], P('tp', 'inst'), may hold values from -0.29882812 to 0.29882812
Outputs:
- updated: bfloat16 [256, 16384], P('tp', 'inst')
Inputs may be any that keep to these rules, and one draw needn't show every extreme that they name: Lent range s serves request lent_req[s], which is never homed on the instance that holds range s. Every instance holds exactly 1 lent range serving requests of each other home instance.
All inputs are finite; a program needn't handle non-finite values.
Results may differ from a plain program's by a relative error of at most 0.0051.
Values may be sent and summed in bfloat16 or wider, within the bound.
No kernel may reach another device: no remote copies, remote signals or barrier semaphores. Data moves between devices by JAX's collectives and lax.ppermute only.
A program may use at most 64 MiB of HBM per device.

v0:
```python
import math

import jax
import jax.numpy as jnp
from jax import lax
from jax.experimental import pallas as pl
from jax.experimental.pallas import tpu as pltpu
from jax.sharding import Mesh, PartitionSpec as P

VERY_LOW = -1e30
ABSENT = 64.0
SCALE = 1.0 / math.sqrt(128.0)
F32 = jnp.float32
BF16 = jnp.bfloat16
NT = (((1,), (1,)), ((), ()))
TN = (((0,), (0,)), ((), ()))
NN = (((1,), (0,)), ((), ()))
INST = ("y", "zh", "zp")
PARAMS = pltpu.CompilerParams(vmem_limit_bytes=16 * 2**20)
SMEM = pl.BlockSpec(memory_space=pltpu.SMEM)
ANY = pl.BlockSpec(memory_space=pl.ANY)
VMEM = pl.BlockSpec(memory_space=pltpu.VMEM)


def dot(a, b, dims):
    return lax.dot_general(a, b, dims, preferred_element_type=F32)


def iota(shape, axis):
    return lax.broadcasted_iota(jnp.int32, shape, axis)


def halves(x):
    high = x.astype(BF16)
    return high, (x - high.astype(F32)).astype(BF16)


def ask_kernel(
    here_ref, table_ref, q_ref, weight_ref, done_ref, asked_ref, req_ref, sent_ref
):
    first = pl.multiple_of((1 - lax.axis_index("zp")) * 1024, 1024)
    sent_ref[...] = weight_ref[pl.ds(first, 1024)]
    here = here_ref[0]
    table = table_ref[...]
    found = jnp.where((table >> 2) == here, (table & 3) + 1, 0).astype(F32)
    lane = iota((1, 128), 1)
    rows = []
    for j in range(64):
        line, first = divmod(63 * j, 128)
        row = jnp.where(lane >= first, found[line : line + 1], 0.0)
        if first + 63 <= 128:
            row = jnp.where(lane < first + 63, row, 0.0)
        else:
            row = jnp.where(lane < first + 63 - 128, found[line + 1 : line + 2], row)
        rows.append(row)
    source = jnp.sum(jnp.concatenate(rows, axis=0), axis=1, keepdims=True) - 1.0
    source = jnp.broadcast_to(source, (64, 128))
    query = [q_ref[r].astype(F32) for r in range(4)]
    for g in range(8):
        rows = []
        for j in range(8 * g, 8 * g + 8):
            s = jnp.broadcast_to(source[j : j + 1], (16, 128))
            picked = jnp.where(s == 1.0, query[1], query[0])
            picked = jnp.where(s == 2.0, query[2], picked)
            rows.append(jnp.where(s == 3.0, query[3], picked))
        asked_ref[g] = jnp.concatenate(rows, axis=0).T.astype(BF16)
    group = iota((8, 128), 1) >> 4
    split = source.reshape(8, 8, 128)
    req = jnp.zeros((8, 128), F32)
    for n in range(8):
        req = jnp.where(group == n, split[:, n], req)
    req_ref[...] = req


def pack_kernel(
    req_ref, len_ref, k_ref, v_ref, out_ref, done_ref,
    req_in, len_in, k_in, v_in, keys_ref, values_ref, sems
):
    loads = [
        pltpu.make_async_copy(source, target, sems.at[i])
        for i, (source, target) in enumerate(
            [(req_ref, req_in), (len_ref, len_in), (k_ref, k_in), (v_ref, v_in)]
        )
    ]
    for load in loads:
        load.start()
    here = lax.axis_index(INST)
    done_ref[...] = jnp.zeros((8, 128), F32)
    token = iota((32, 128), 0)
    keys_ref[here] = jnp.full((32, 128), ABSENT, F32).astype(BF16)
    values_ref[here] = jnp.zeros((32, 128), F32).astype(BF16)
    for load in loads[:3]:
        load.wait()
    for s in range(63):
        keys = jnp.where(token < len_in[s], k_in[s].astype(F32), ABSENT)
        keys_ref[req_in[63 * here + s] >> 2] = keys.astype(BF16)
    send_keys = pltpu.make_async_copy(keys_ref, out_ref.at[:, pl.ds(0, 32)], sems.at[4])
    send_keys.start()
    loads[3].wait()
    for s in range(63):
        values_ref[req_in[63 * here + s] >> 2] = v_in[s]
    send_values = pltpu.make_async_copy(values_ref, out_ref.at[:, pl.ds(32, 32)], sems.at[5])
    send_values.start()
    send_keys.wait()
    send_values.wait()


def home_kernel(
    len_ref, q_ref, nk_ref, nv_ref, k_ref, v_ref, residual_ref, out_ref, stat_ref, base_ref
):
    query = q_ref[...].reshape(64, 128)
    query = jnp.concatenate([query, query], axis=0)
    owner = (iota((256, 128), 1) >> 4) & 3
    token = iota((256, 128), 0)
    scores = jnp.zeros((256, 128), F32)
    length = jnp.zeros((256, 128), jnp.int32)
    for r in range(4):
        scores = jnp.where(owner == r, dot(k_ref[r], query, NT), scores)
        length = jnp.where(owner == r, len_ref[r], length)
    scores = jnp.where(token < length, scores * SCALE, VERY_LOW)
    mine = ((iota((4, 128), 1) >> 4) & 3) == iota((4, 128), 0)
    fresh = dot(nk_ref[...], query, NT) * SCALE
    fresh = jnp.sum(jnp.where(mine, fresh, 0.0), axis=0, keepdims=True)
    top = jnp.maximum(jnp.max(scores, axis=0, keepdims=True), fresh)
    weights = jnp.exp(scores - top)
    own = jnp.exp(fresh - top)
    total = jnp.sum(weights, axis=0, keepdims=True) + own
    mixed = dot(jnp.where(mine, own, 0.0).astype(BF16), nv_ref[...], TN)
    for r in range(4):
        mixed += dot(jnp.where(owner == r, weights, 0.0).astype(BF16), v_ref[r], TN)
    out_ref[...] = mixed[:64]
    stat_ref[...] = jnp.concatenate([top, total], axis=0)
    base_ref[...] = residual_ref[...].astype(F32)


def attend_kernel(q_ref, req_ref, stat_ref, home_ref, recv_ref, out_ref, mixed_ref):
    owner = iota((32, 128), 1) >> 4
    far_tops, far_totals = [], []
    for g in range(8):
        here = pl.ds(8 * g, 8)
        keys = recv_ref[here, :32, :].reshape(256, 128)
        raw = dot(keys, q_ref[g], NN)
        mark = keys.astype(F32)
        scores, marks = raw[:32], mark[:32]
        for j in range(1, 8):
            scores = jnp.where(owner == j, raw[32 * j : 32 * j + 32], scores)
            marks = jnp.where(owner == j, mark[32 * j : 32 * j + 32], marks)
        scores = jnp.where(marks < 0.5 * ABSENT, scores * SCALE, VERY_LOW)
        top = jnp.max(scores, axis=0, keepdims=True)
        weights = jnp.exp(scores - top)
        far_tops.append(top)
        far_totals.append(jnp.sum(weights, axis=0, keepdims=True))
        blocks = jnp.concatenate(
            [jnp.where(owner == j, weights, 0.0) for j in range(8)], axis=0
        ).astype(BF16)
        values = recv_ref[here, 32:, :].reshape(256, 128)
        mixed_ref[128 * g : 128 * g + 128] = dot(blocks, values, TN)
    far_top = jnp.concatenate(far_tops, axis=0)
    far_total = jnp.concatenate(far_totals, axis=0)
    near_top, near_total = stat_ref[0:1], stat_ref[1:2]
    which = iota((1, 128), 1) >> 4
    req = req_ref[...]
    tops = []
    for r in range(4):
        t = jnp.max(jnp.where(req == r, far_top, VERY_LOW), axis=0, keepdims=True)
        tops.append(jnp.maximum(t, jnp.where(which == r, near_top, VERY_LOW)))
    peak = jnp.concatenate(tops, axis=0)
    for shift in (16, 32, 64):
        peak = jnp.maximum(peak, pltpu.roll(peak, shift, 1))
    far_w, near_w, totals = [], [], []
    for r in range(4):
        p = peak[r : r + 1]
        f = jnp.where(req == r, jnp.exp(far_top - p), 0.0)
        n = jnp.where(which == r, jnp.exp(near_top - p), 0.0)
        far_w.append(f)
        near_w.append(n)
        totals.append(jnp.sum(f * far_total, axis=0, keepdims=True) + n * near_total)
    total = jnp.concatenate(totals, axis=0)
    for shift in (16, 32, 64):
        total = total + pltpu.roll(total, shift, 1)
    scale = 1.0 / total
    same = (iota((16, 128), 1) & 15) == iota((16, 128), 0)

    def spread_rows(rows):
        return halves(jnp.concatenate([jnp.where(same, row, 0.0) for row in rows], axis=0))

    high, low = spread_rows([near_w[r] * scale[r : r + 1] for r in range(4)])
    home_high, home_low = halves(home_ref[...])
    acc = dot(high[:, :64], home_high, NN) + dot(high[:, :64], home_low, NN)
    acc += dot(low[:, :64], home_high, NN)
    far_w = [far_w[r] * scale[r : r + 1] for r in range(4)]
    for g in range(8):
        high, low = spread_rows([far_w[r][g : g + 1] for r in range(4)])
        mixed_high, mixed_low = halves(mixed_ref[128 * g : 128 * g + 128])
        acc += dot(high, mixed_high, NN) + dot(high, mixed_low, NN) + dot(low, mixed_high, NN)
    lower = jnp.concatenate([acc[16 * r : 16 * r + 8] for r in range(4)], axis=0)
    upper = jnp.concatenate([acc[16 * r + 8 : 16 * r + 16] for r in range(4)], axis=0)
    split = jnp.concatenate([lower, upper], axis=0).astype(BF16).reshape(1, 2, 32, 128)
    out_ref[...] = jnp.broadcast_to(split, (32, 2, 32, 128)).reshape(64, 32, 128)


def join_kernel(mine_ref, received_ref, out_ref):
    zp = lax.axis_index("zp")
    out_ref[zp] = mine_ref[pl.ds(pl.multiple_of(zp * 1024, 1024), 1024)]
    out_ref[1 - zp] = received_ref[...]


def project_kernel(rows_ref, weight_ref, out_ref, wide_ref):
    q = iota((256, 256), 0)
    p = iota((256, 256), 1)
    move = p == 32 * ((q >> 2) & 7) + 8 * (q & 3) + (q >> 5)
    move = move.astype(F32).astype(BF16)
    for b in range(8):
        moved = dot(move, rows_ref[8 * b : 8 * b + 8].reshape(256, 128), NN).astype(BF16)
        for h in range(8):
            wide_ref[32 * b : 32 * b + 32, 128 * h : 128 * h + 128] = moved[32 * h : 32 * h + 32]
    wide = wide_ref[...]
    for c in range(2):
        out_ref[c] = dot(wide, weight_ref[c], NN).astype(BF16).reshape(8, 32, 256)


def finish_kernel(sums_ref, base_ref, out_ref):
    total = base_ref[...]
    for s in range(16):
        total = total + sums_ref[s].astype(F32)
    out_ref[...] = total.astype(BF16)


def body(
    queries,
    new_keys,
    new_values,
    home_keys,
    home_values,
    home_len,
    lent_keys,
    lent_values,
    lent_req,
    lent_len,
    out_weight,
    residual,
):
    here = lax.axis_index(INST)
    packed, done = pl.pallas_call(
        pack_kernel,
        out_shape=(
            jax.ShapeDtypeStruct((64, 64, 128), BF16),
            jax.ShapeDtypeStruct((8, 128), F32),
        ),
        in_specs=[ANY] * 4,
        out_specs=(ANY, VMEM),
        scratch_shapes=[
            pltpu.SMEM((4032,), jnp.int32),
            pltpu.SMEM((63,), jnp.int32),
            pltpu.VMEM((63, 32, 128), BF16),
            pltpu.VMEM((63, 32, 128), BF16),
            pltpu.VMEM((64, 32, 128), BF16),
            pltpu.VMEM((64, 32, 128), BF16),
            pltpu.SemaphoreType.DMA((6,)),
        ],
        name="pack_lent",
    )(
        lent_req,
        lent_len,
        lent_keys.reshape(63, 32, 128),
        lent_values.reshape(63, 32, 128),
    )
    recv = lax.all_to_all(packed, INST, split_axis=0, concat_axis=0, tiled=True)
    asked, req, sent = pl.pallas_call(
        ask_kernel,
        out_shape=(
            jax.ShapeDtypeStruct((8, 128, 128), BF16),
            jax.ShapeDtypeStruct((8, 128), F32),
            jax.ShapeDtypeStruct((1024, 256), BF16),
        ),
        in_specs=[SMEM, VMEM, VMEM, VMEM, ANY],
        out_specs=(VMEM,) * 3,
        compiler_params=PARAMS,
        name="ask_queries",
    )(
        here.reshape(1),
        jnp.pad(lent_req, (0, 64), constant_values=-4).reshape(32, 128),
        queries,
        out_weight,
        done,
    )
    received = lax.ppermute(sent, "zp", [(0, 1), (1, 0)])
    home_out, home_stat, base = pl.pallas_call(
        home_kernel,
        out_shape=(
            jax.ShapeDtypeStruct((64, 128), F32),
            jax.ShapeDtypeStruct((2, 128), F32),
            jax.ShapeDtypeStruct((32, 256), F32),
        ),
        in_specs=[SMEM] + [VMEM] * 6,
        out_specs=(VMEM,) * 3,
        compiler_params=PARAMS,
        name="home_part",
    )(
        home_len,
        queries,
        new_keys.reshape(4, 128),
        new_values.reshape(4, 128),
        home_keys.reshape(4, 256, 128),
        home_values.reshape(4, 256, 128),
        residual,
    )
    copies = pl.pallas_call(
        attend_kernel,
        out_shape=jax.ShapeDtypeStruct((64, 32, 128), BF16),
        in_specs=[VMEM] * 5,
        out_specs=VMEM,
        scratch_shapes=[pltpu.VMEM((1024, 128), F32)],
        compiler_params=PARAMS,
        name="attend",
    )(asked, req, home_stat, home_out, recv)
    rows = lax.all_to_all(copies, INST, split_axis=0, concat_axis=0, tiled=True)
    weights = pl.pallas_call(
        join_kernel,
        out_shape=jax.ShapeDtypeStruct((2, 1024, 256), BF16),
        in_specs=[VMEM, VMEM],
        out_specs=VMEM,
        compiler_params=PARAMS,
        cost_estimate=pl.CostEstimate(flops=10**11, bytes_accessed=2**21, transcendentals=0),
        name="join_weights",
    )(out_weight, received)
    partial = pl.pallas_call(
        project_kernel,
        out_shape=jax.ShapeDtypeStruct((2, 8, 32, 256), BF16),
        in_specs=[VMEM, VMEM],
        out_specs=VMEM,
        scratch_shapes=[pltpu.VMEM((256, 1024), BF16)],
        compiler_params=PARAMS,
        name="project",
    )(rows, weights)
    sums = lax.all_to_all(
        partial.reshape(16, 32, 256), ("zp", "tp"), split_axis=0, concat_axis=0, tiled=True
    )
    return pl.pallas_call(
        finish_kernel,
        out_shape=jax.ShapeDtypeStruct((32, 256), BF16),
        in_specs=[VMEM, VMEM],
        out_specs=VMEM,
        compiler_params=PARAMS,
        name="finish",
    )(sums, base)


def solution(mesh):
    placed = (
        P(INST, "tp", None),
        P(INST, "tp", None),
        P(INST, "tp", None),
        P(INST, None, "tp", None),
        P(INST, None, "tp", None),
        P(INST),
        P(INST, None, "tp", None),
        P(INST, None, "tp", None),
        P(),
        P(INST),
        P("tp", INST),
        P("tp", INST),
    )
    fine = Mesh(mesh.devices.reshape(8, 4, 2, 8), INST + ("tp",))
    return jax.shard_map(
        body, mesh=fine, in_specs=placed, out_specs=P("tp", INST), check_vma=False
    )
```

profile of v0, /device:TPU:1, one launch (start us, length us, event | category | flops | bytes accessed | tf_op | source)
XLA Modules:
  0.0 92.5 jit_solution(6288578841028314088)
XLA Ops:
  0.0 2.8 %pack_lent.1 = (bf16[64,64,128]{2,1,0:T(8,128)(2,1)}, f32[8,128]{1,0:T(8,128)}) custom-call(s32[4032]{0:T(1024)} %req_ref.1, s32[63]{0:T(128)} %len_ref.2, bf16[63,32,128]{2,1,0:T(8,128)(2,1)} %bitcast.15, bf16[63,32,128]{2,1,0:T(8,128)(2,1)} %bitcast.16), custom_call_target="tpu_custom_call" | custom-call | tf_op jit(solution)/shard_map/pack_lent/pallas_call | solution.py:244
  2.8 0.0 copy-start
  2.9 17.3 %all-to-all-start = ((bf16[64,64,128]{2,1,0:T(8,128)(2,1)}), bf16[64,64,128]{2,1,0:T(8,128)(2,1)S(1)}, u32[]{:S(2)}, u32[]{:S(2)}) async-start(bf16[64,64,128]{2,1,0:T(8,128)(2,1)} %get-tuple-element.18), calls=%async_computation | async-start | bytes 2097152 | tf_op jit(solution)/shard_map/all_to_all | solution.py:268
  20.1 0.0 copy-start.9
  20.2 0.7 copy-done.9
  20.9 0.0 copy-start.3
  20.9 0.0 copy-start.5
  20.9 0.0 copy-done
  20.9 0.7 copy-done.3
  21.6 0.0 copy-done.5
  21.6 0.0 copy-start.1
  21.6 0.0 copy-start.2
  21.6 0.0 copy-start.4
  21.6 0.0 copy-start.7
  21.6 0.3 ask_queries.1
  21.9 2.9 %collective-permute-start = (bf16[1024,256]{1,0:T(8,128)(2,1)S(1)}, bf16[1024,256]{1,0:T(8,128)(2,1)}, u32[]{:S(2)}, u32[]{:S(2)}) collective-permute-start(bf16[1024,256]{1,0:T(8,128)(2,1)S(1)} %get-tuple-element.19), channel_id=1, source_target_pairs={{0,8},{8,0},{1,9},{9,1},{2,10},{10,2},{3,11},{11,3},{4,12},{12,4},... | collective-permute-start | bytes 1572872 | tf_op jit(solution)/shard_map/ppermute | solution.py:287
  24.8 0.0 copy-start.6
  24.8 0.0 copy-start.8
  24.8 0.0 copy-done.1
  24.9 0.0 copy-done.2
  24.9 0.0 copy-done.4
  24.9 0.0 copy-done.7
  24.9 0.6 copy-done.6
  25.5 0.0 copy-done.8
  25.5 1.1 %home_part.1 = (f32[64,128]{1,0:T(8,128)S(1)}, f32[2,128]{1,0:T(2,128)S(1)}, f32[32,256]{1,0:T(8,128)S(1)}) custom-call(s32[4]{0:T(128)S(1)} %copy-done.8, bf16[4,16,128]{2,1,0:T(8,128)(2,1)S(1)} %copy-done.3, bf16[4,128]{1,0:T(4,128)(2,1)S(1)} %bitcast.13, bf16[4,128]{1,0:T(4,128)(2,1)S(1)} %bitcast.14, bf16[4,256,128]{2,1,0:T(8,128)(2,1)S(1)} %bitcast.11, ...), custom_call_target="tpu_custom_call" | custom-call | tf_op jit(solution)/shard_map/home_part/pallas_call | solution.py:288
  26.6 20.3 %all-to-all-done.recv_ref = bf16[64,64,128]{2,1,0:T(8,128)(2,1)S(1)} async-done(((bf16[64,64,128]{2,1,0:T(8,128)(2,1)}), bf16[64,64,128]{2,1,0:T(8,128)(2,1)S(1)}, u32[]{:S(2)}, u32[]{:S(2)}) %all-to-all-start) | async-done | bytes 1048608 | tf_op jit(solution)/shard_map/all_to_all | solution.py:268
  46.9 3.3 %attend.1 = bf16[64,32,128]{2,1,0:T(8,128)(2,1)} custom-call(bf16[8,128,128]{2,1,0:T(8,128)(2,1)S(1)} %get-tuple-element.14.q_ref, f32[8,128]{1,0:T(8,128)S(1)} %get-tuple-element.15.req_ref, f32[2,128]{1,0:T(2,128)S(1)} %get-tuple-element.16.stat_ref, f32[64,128]{1,0:T(8,128)S(1)} %get-tuple-element.17.home_ref, bf16[64,64,128]{2,1,0:T(8,128)(2,1)S(1)} %all-to-all-done.recv_ref), custom_call_target="tpu_custom_call" | custom-call | tf_op jit(solution)/shard_map/attend/pallas_call | solution.py:308
  50.2 9.0 %all-to-all-start.1 = ((bf16[64,32,128]{2,1,0:T(8,128)(2,1)}), bf16[64,32,128]{2,1,0:T(8,128)(2,1)S(1)}, u32[]{:S(2)}, u32[]{:S(2)}) async-start(bf16[64,32,128]{2,1,0:T(8,128)(2,1)} %attend.1), calls=%async_computation.1 | async-start | bytes 1048576 | tf_op jit(solution)/shard_map/all_to_all | solution.py:317
  59.2 0.0 collective-permute-done.received_ref
  59.2 1.1 %join_weights.1.weight_ref = bf16[2,1024,256]{2,1,0:T(8,128)(2,1)S(1)} custom-call(bf16[2048,256]{1,0:T(8,128)(2,1)S(1)} %copy-done, bf16[1024,256]{1,0:T(8,128)(2,1)} %collective-permute-done.received_ref), custom_call_target="tpu_custom_call" | custom-call | flops 99999997952 | bytes 2097152 | tf_op jit(solution)/shard_map/join_weights/pallas_call | solution.py:318
  60.3 15.1 %all-to-all-done.1.rows_ref = bf16[64,32,128]{2,1,0:T(8,128)(2,1)S(1)} async-done(((bf16[64,32,128]{2,1,0:T(8,128)(2,1)}), bf16[64,32,128]{2,1,0:T(8,128)(2,1)S(1)}, u32[]{:S(2)}, u32[]{:S(2)}) %all-to-all-start.1) | async-done | bytes 524320 | tf_op jit(solution)/shard_map/all_to_all | solution.py:317
  75.4 0.7 project.1
  76.1 15.7 %all_to_all.15.sums_ref = bf16[16,32,256]{2,1,0:T(8,128)(2,1)S(1)} all-to-all(bf16[16,32,256]{2,1,0:T(8,128)(2,1)S(1)} %bitcast.10), channel_id=1, replica_groups=mesh['y'=8,'zh'=4,'zp'=2,'tp'=8] {'zp','tp'}, dimensions={0} | all-to-all | bytes 524288 | tf_op jit(solution)/shard_map/all_to_all | solution.py:336
  91.8 0.6 finish.1
  (1 shorter events, 0.0 us)
Async XLA Ops:
  2.8 18.0 %copy-start = (bf16[2048,256]{1,0:T(8,128)(2,1)S(1)}, bf16[2048,256]{1,0:T(8,128)(2,1)}, u32[]{:S(2)}) copy-start(bf16[2048,256]{1,0:T(8,128)(2,1)} %mine_ref.1) | copy-start | bytes 3145732
  2.9 44.0 %all-to-all-start = ((bf16[64,64,128]{2,1,0:T(8,128)(2,1)}), bf16[64,64,128]{2,1,0:T(8,128)(2,1)S(1)}, u32[]{:S(2)}, u32[]{:S(2)}) async-start(bf16[64,64,128]{2,1,0:T(8,128)(2,1)} %get-tuple-element.18), calls=%async_computation | async-start | bytes 2097152 | tf_op jit(solution)/shard_map/all_to_all | solution.py:268
  20.1 0.7 copy-start.9
  20.9 0.7 copy-start.3
  20.9 0.7 copy-start.5
  21.6 3.3 %copy-start.1 = (bf16[4,256,1,128]{3,1,2,0:T(8,128)(2,1)S(1)}, bf16[4,256,1,128]{3,1,2,0:T(8,128)(2,1)}, u32[]{:S(2)}) copy-start(bf16[4,256,1,128]{3,1,2,0:T(8,128)(2,1)} %param.15) | copy-start | bytes 786436
  21.6 3.3 %copy-start.2 = (bf16[4,256,1,128]{3,1,2,0:T(8,128)(2,1)S(1)}, bf16[4,256,1,128]{3,1,2,0:T(8,128)(2,1)}, u32[]{:S(2)}) copy-start(bf16[4,256,1,128]{3,1,2,0:T(8,128)(2,1)} %param.16) | copy-start | bytes 786436
  21.6 3.3 %copy-start.4 = (bf16[32,256]{1,0:T(8,128)(2,1)S(1)}, bf16[32,256]{1,0:T(8,128)(2,1)}, u32[]{:S(2)}) copy-start(bf16[32,256]{1,0:T(8,128)(2,1)} %residual_ref.1) | copy-start | bytes 49156
  21.6 3.3 %copy-start.7 = (bf16[4,1,128]{2,0,1:T(4,128)(2,1)S(1)}, bf16[4,1,128]{2,0,1:T(4,128)(2,1)}, u32[]{:S(2)}) copy-start(bf16[4,1,128]{2,0,1:T(4,128)(2,1)} %param.14) | copy-start | bytes 3076
  21.9 37.3 %collective-permute-start = (bf16[1024,256]{1,0:T(8,128)(2,1)S(1)}, bf16[1024,256]{1,0:T(8,128)(2,1)}, u32[]{:S(2)}, u32[]{:S(2)}) collective-permute-start(bf16[1024,256]{1,0:T(8,128)(2,1)S(1)} %get-tuple-element.19), channel_id=1, source_target_pairs={{0,8},{8,0},{1,9},{9,1},{2,10},{10,2},{3,11},{11,3},{4,12},{12,4},... | collective-permute-start | bytes 1572872 | tf_op jit(solution)/shard_map/ppermute | solution.py:287
  24.8 0.7 copy-start.6
  24.8 0.7 copy-start.8
  50.2 25.2 %all-to-all-start.1 = ((bf16[64,32,128]{2,1,0:T(8,128)(2,1)}), bf16[64,32,128]{2,1,0:T(8,128)(2,1)S(1)}, u32[]{:S(2)}, u32[]{:S(2)}) async-start(bf16[64,32,128]{2,1,0:T(8,128)(2,1)} %attend.1), calls=%async_computation.1 | async-start | bytes 1048576 | tf_op jit(solution)/shard_map/all_to_all | solution.py:317
where the time goes:
time: 93.2 us; the launch traced here: 92.5 us
  waiting for transfers between devices  35.4 us (38%)
  starting transfers between devices  29.2 us (31%)
  blocking collectives  15.7 us (17%)
  Pallas kernels  9.97 us (11%)
  local copies, waits for them, and re-layouts  2.06 us (2%)
    all_to_all x1, waiting for transfers between devices, body(): recv = lax.all_to_all(packed, INST, split_axis=0, concat_axis=0, tiled=True)  20.3 us
    all_to_all x1, starting transfers between devices, body(): recv = lax.all_to_all(packed, INST, split_axis=0, concat_axis=0, tiled=True)  17.3 us
    all_to_all x1, blocking collectives, body(): lax.all_to_all(partial.reshape(16, 32, 256), ('zp', 'tp'), split_axis=0,...  15.7 us
    all_to_all x1, waiting for transfers between devices, body(): rows = lax.all_to_all(copies, INST, split_axis=0, concat_axis=0, tiled=True)  15.1 us
    all_to_all x1, starting transfers between devices, body(): rows = lax.all_to_all(copies, INST, split_axis=0, concat_axis=0, tiled=True)  8.99 us
    pallas_call x1, Pallas kernels, body(): pl.pallas_call(attend_kernel, out_shape=jax.ShapeDtypeStruct((64, 32, 128...  3.29 us
    ppermute x1, starting transfers between devices, body(): received = lax.ppermute(sent, 'zp', [(0, 1), (1, 0)])  2.92 us
    pallas_call x1, Pallas kernels, body(): pl.pallas_call(pack_kernel, out_shape=(jax.ShapeDtypeStruct((64, 64, 128)...  2.83 us
  transfers between devices with their start and end apart: 3, of which 2 were waited for; matrix products, arithmetic and copies ran while one was open for 0% of the time, Pallas kernels for 6%

commit v1 on v0

--- a/solution.py
+++ b/solution.py
@@ -16,6 +16,8 @@
 TN = (((0,), (0,)), ((), ()))
 NN = (((1,), (0,)), ((), ()))
 INST = ("y", "zh", "zp")
+FIRST = 52
+ORDER = [[(FIRST + k) % 64 for k in range(64)]]
 PARAMS = pltpu.CompilerParams(vmem_limit_bytes=16 * 2**20)
 SMEM = pl.BlockSpec(memory_space=pltpu.SMEM)
 ANY = pl.BlockSpec(memory_space=pl.ANY)
@@ -36,7 +38,7 @@
 
 
 def ask_kernel(
-    here_ref, table_ref, q_ref, weight_ref, done_ref, asked_ref, req_ref, sent_ref
+    here_ref, table_ref, q_ref, weight_ref, packed_ref, asked_ref, req_ref, sent_ref
 ):
     first = pl.multiple_of((1 - lax.axis_index("zp")) * 1024, 1024)
     sent_ref[...] = weight_ref[pl.ds(first, 1024)]
@@ -45,7 +47,7 @@
     found = jnp.where((table >> 2) == here, (table & 3) + 1, 0).astype(F32)
     lane = iota((1, 128), 1)
     rows = []
-    for j in range(64):
+    for j in ORDER[0]:
         line, first = divmod(63 * j, 128)
         row = jnp.where(lane >= first, found[line : line + 1], 0.0)
         if first + 63 <= 128:
@@ -73,7 +75,7 @@
 
 
 def pack_kernel(
-    req_ref, len_ref, k_ref, v_ref, out_ref, done_ref,
+    req_ref, len_ref, k_ref, v_ref, out_ref,
     req_in, len_in, k_in, v_in, keys_ref, values_ref, sems
 ):
     loads = [
@@ -85,20 +87,20 @@
     for load in loads:
         load.start()
     here = lax.axis_index(INST)
-    done_ref[...] = jnp.zeros((8, 128), F32)
+    place = (here - FIRST) & 63
     token = iota((32, 128), 0)
-    keys_ref[here] = jnp.full((32, 128), ABSENT, F32).astype(BF16)
-    values_ref[here] = jnp.zeros((32, 128), F32).astype(BF16)
+    keys_ref[place] = jnp.full((32, 128), ABSENT, F32).astype(BF16)
+    values_ref[place] = jnp.zeros((32, 128), F32).astype(BF16)
     for load in loads[:3]:
         load.wait()
     for s in range(63):
         keys = jnp.where(token < len_in[s], k_in[s].astype(F32), ABSENT)
-        keys_ref[req_in[63 * here + s] >> 2] = keys.astype(BF16)
+        keys_ref[((req_in[63 * here + s] >> 2) - FIRST) & 63] = keys.astype(BF16)
     send_keys = pltpu.make_async_copy(keys_ref, out_ref.at[:, pl.ds(0, 32)], sems.at[4])
     send_keys.start()
     loads[3].wait()
     for s in range(63):
-        values_ref[req_in[63 * here + s] >> 2] = v_in[s]
+        values_ref[((req_in[63 * here + s] >> 2) - FIRST) & 63] = v_in[s]
     send_values = pltpu.make_async_copy(values_ref, out_ref.at[:, pl.ds(32, 32)], sems.at[5])
     send_values.start()
     send_keys.wait()
@@ -241,14 +243,11 @@
     residual,
 ):
     here = lax.axis_index(INST)
-    packed, done = pl.pallas_call(
+    packed = pl.pallas_call(
         pack_kernel,
-        out_shape=(
-            jax.ShapeDtypeStruct((64, 64, 128), BF16),
-            jax.ShapeDtypeStruct((8, 128), F32),
-        ),
+        out_shape=jax.ShapeDtypeStruct((64, 64, 128), BF16),
         in_specs=[ANY] * 4,
-        out_specs=(ANY, VMEM),
+        out_specs=ANY,
         scratch_shapes=[
             pltpu.SMEM((4032,), jnp.int32),
             pltpu.SMEM((63,), jnp.int32),
@@ -265,7 +264,9 @@
         lent_keys.reshape(63, 32, 128),
         lent_values.reshape(63, 32, 128),
     )
-    recv = lax.all_to_all(packed, INST, split_axis=0, concat_axis=0, tiled=True)
+    recv = lax.all_to_all(
+        packed, INST, split_axis=0, concat_axis=0, tiled=True, axis_index_groups=ORDER
+    )
     asked, req, sent = pl.pallas_call(
         ask_kernel,
         out_shape=(
@@ -282,7 +283,7 @@
         jnp.pad(lent_req, (0, 64), constant_values=-4).reshape(32, 128),
         queries,
         out_weight,
-        done,
+        packed,
     )
     received = lax.ppermute(sent, "zp", [(0, 1), (1, 0)])
     home_out, home_stat, base = pl.pallas_call(

time: 93.2 us -> 92.2 us (0.989)
  waiting for transfers between devices: 35.4 us -> 28.5 us
  starting transfers between devices: 29.2 us -> 32.2 us
  blocking collectives: 15.7 us -> 17.6 us
  local copies, waits for them, and re-layouts: 2.06 us -> 3.89 us
    all_to_all x1, waiting for transfers between devices: 20.3 us -> 15.9 us  [body(): lax.all_to_all(packed, INST, split_axis=0, concat_axis=0, tiled=True, axi...]
    all_to_all x1, starting transfers between devices: 17.3 us -> 19.8 us  [body(): lax.all_to_all(packed, INST, split_axis=0, concat_axis=0, tiled=True, axi...]
    all_to_all x1, waiting for transfers between devices: 15.1 us -> 12.6 us  [body(): rows = lax.all_to_all(copies, INST, split_axis=0, concat_axis=0, tiled=True)]
    all_to_all x1, blocking collectives: 15.7 us -> 17.6 us  [body(): lax.all_to_all(partial.reshape(16, 32, 256), ('zp', 'tp'), split_axis=0,...]
    unnamed x20 -> x24, local copies, waits for them, and re-layouts: 2.06 us -> 3.89 us
    all_to_all x1, starting transfers between devices: 8.99 us -> 10.2 us  [body(): rows = lax.all_to_all(copies, INST, split_axis=0, concat_axis=0, tiled=True)]
    pallas_call x1, Pallas kernels: 1.13 us -> 0.09 us  [body(): pl.pallas_call(join_kernel, out_shape=jax.ShapeDtypeStruct((2, 1024, 256)...]
where the time goes in v1:
time: 92.2 us; the launch traced here: 91.5 us
  starting transfers between devices  32.2 us (35%)
  waiting for transfers between devices  28.5 us (31%)
  blocking collectives  17.6 us (19%)
  Pallas kernels  9.14 us (10%)
  local copies, waits for them, and re-layouts  3.89 us (4%)
    all_to_all x1, starting transfers between devices, body(): lax.all_to_all(packed, INST, split_axis=0, concat_axis=0, tiled=True, axi...  19.8 us
    all_to_all x1, blocking collectives, body(): lax.all_to_all(partial.reshape(16, 32, 256), ('zp', 'tp'), split_axis=0,...  17.6 us
    all_to_all x1, waiting for transfers between devices, body(): lax.all_to_all(packed, INST, split_axis=0, concat_axis=0, tiled=True, axi...  15.9 us
    all_to_all x1, waiting for transfers between devices, body(): rows = lax.all_to_all(copies, INST, split_axis=0, concat_axis=0, tiled=True)  12.6 us
    all_to_all x1, starting transfers between devices, body(): rows = lax.all_to_all(copies, INST, split_axis=0, concat_axis=0, tiled=True)  10.2 us
    unnamed x24, local copies, waits for them, and re-layouts  3.89 us
    pallas_call x1, Pallas kernels, body(): pl.pallas_call(attend_kernel, out_shape=jax.ShapeDtypeStruct((64, 32, 128...  3.3 us
    pallas_call x1, Pallas kernels, body(): pl.pallas_call(pack_kernel, out_shape=jax.ShapeDtypeStruct((64, 64, 128),...  2.24 us
  transfers between devices with their start and end apart: 3, of which 2 were waited for; matrix products, arithmetic and copies ran while one was open for 0% of the time, Pallas kernels for 6%

profile of v1, /device:TPU:1, one launch (start us, length us, event | category | flops | bytes accessed | tf_op | source)
XLA Modules:
  0.0 91.5 jit_solution(4739355149357388022)
XLA Ops:
  0.0 2.2 %pack_lent.1.packed_ref = bf16[64,64,128]{2,1,0:T(8,128)(2,1)} custom-call(s32[4032]{0:T(1024)} %req_ref.1, s32[63]{0:T(128)} %len_ref.2, bf16[63,32,128]{2,1,0:T(8,128)(2,1)} %bitcast.15, bf16[63,32,128]{2,1,0:T(8,128)(2,1)} %bitcast.16), custom_call_target="tpu_custom_call" | custom-call | tf_op jit(solution)/shard_map/pack_lent/pallas_call | solution.py:246
  2.3 0.0 copy-start
  2.3 0.0 copy-start.1
  2.3 19.8 %all-to-all-start = ((bf16[64,64,128]{2,1,0:T(8,128)(2,1)}), bf16[64,64,128]{2,1,0:T(8,128)(2,1)S(1)}, u32[]{:S(2)}, u32[]{:S(2)}) async-start(bf16[64,64,128]{2,1,0:T(8,128)(2,1)} %pack_lent.1.packed_ref), calls=%async_computation | async-start | bytes 2097152 | tf_op jit(solution)/shard_map/all_to_all | solution.py:267
  22.1 0.0 copy-start.11
  22.1 0.7 copy-done.11
  22.8 0.0 copy-start.4
  22.8 0.0 copy-done
  22.8 0.0 copy-done.1
  22.8 0.7 copy-done.4
  23.5 0.0 copy-start.2
  23.5 0.0 copy-start.3
  23.5 0.0 copy-start.5
  23.5 0.0 copy-start.7
  23.5 1.1 %ask_queries.1 = (bf16[8,128,128]{2,1,0:T(8,128)(2,1)S(1)}, f32[8,128]{1,0:T(8,128)S(1)}, bf16[1024,256]{1,0:T(8,128)(2,1)}) custom-call(s32[1]{0:T(128)} %bitcast.here_ref, s32[32,128]{1,0:T(8,128)S(1)} %pad_bitcast_fusion.table_ref, bf16[4,16,128]{2,1,0:T(8,128)(2,1)S(1)} %copy-done.4, bf16[2048,256]{1,0:T(8,128)(2,1)S(1)} %copy-done.1, ...), custom_call_target="tpu_custom_call" | custom-call | tf_op jit(solution)/shard_map/ask_queries/pallas_call | solution.py:270
  24.6 2.2 %collective-permute-start = (bf16[1024,256]{1,0:T(8,128)(2,1)}, bf16[1024,256]{1,0:T(8,128)(2,1)S(1)}, u32[]{:S(2)}, u32[]{:S(2)}) collective-permute-start(bf16[1024,256]{1,0:T(8,128)(2,1)} %get-tuple-element.15), channel_id=1, source_target_pairs={{0,8},{8,0},{1,9},{9,1},{2,10},{10,2},{3,11},{11,3},{4,12},{12,4},... | collective-permute-start | bytes 1572872 | tf_op jit(solution)/shard_map/ppermute | solution.py:288
  26.8 0.0 copy-start.6
  26.8 0.0 copy-start.8
  26.8 0.0 copy-done.2
  26.8 0.0 copy-done.3
  26.9 0.0 copy-done.5
  26.9 0.0 copy-done.7
  26.9 0.6 copy-done.6
  27.5 0.0 copy-done.8
  27.5 1.1 %home_part.1 = (f32[64,128]{1,0:T(8,128)S(1)}, f32[2,128]{1,0:T(2,128)S(1)}, f32[32,256]{1,0:T(8,128)S(1)}) custom-call(s32[4]{0:T(128)S(1)} %copy-done.8, bf16[4,16,128]{2,1,0:T(8,128)(2,1)S(1)} %copy-done.4, bf16[4,128]{1,0:T(4,128)(2,1)S(1)} %bitcast.13, bf16[4,128]{1,0:T(4,128)(2,1)S(1)} %bitcast.14, bf16[4,256,128]{2,1,0:T(8,128)(2,1)S(1)} %bitcast.11, ...), custom_call_target="tpu_custom_call" | custom-call | tf_op jit(solution)/shard_map/home_part/pallas_call | solution.py:289
  28.6 15.9 %all-to-all-done.recv_ref = bf16[64,64,128]{2,1,0:T(8,128)(2,1)S(1)} async-done(((bf16[64,64,128]{2,1,0:T(8,128)(2,1)}), bf16[64,64,128]{2,1,0:T(8,128)(2,1)S(1)}, u32[]{:S(2)}, u32[]{:S(2)}) %all-to-all-start) | async-done | bytes 1048608 | tf_op jit(solution)/shard_map/all_to_all | solution.py:267
  44.4 3.3 %attend.1 = bf16[64,32,128]{2,1,0:T(8,128)(2,1)} custom-call(bf16[8,128,128]{2,1,0:T(8,128)(2,1)S(1)} %get-tuple-element.11.q_ref, f32[8,128]{1,0:T(8,128)S(1)} %get-tuple-element.12.req_ref, f32[2,128]{1,0:T(2,128)S(1)} %get-tuple-element.13.stat_ref, f32[64,128]{1,0:T(8,128)S(1)} %get-tuple-element.14.home_ref, bf16[64,64,128]{2,1,0:T(8,128)(2,1)S(1)} %all-to-all-done.recv_ref), custom_call_target="tpu_custom_call" | custom-call | tf_op jit(solution)/shard_map/attend/pallas_call | solution.py:309
  47.7 10.2 %all-to-all-start.1 = ((bf16[64,32,128]{2,1,0:T(8,128)(2,1)}), bf16[64,32,128]{2,1,0:T(8,128)(2,1)S(1)}, u32[]{:S(2)}, u32[]{:S(2)}) async-start(bf16[64,32,128]{2,1,0:T(8,128)(2,1)} %attend.1), calls=%async_computation.1 | async-start | bytes 1048576 | tf_op jit(solution)/shard_map/all_to_all | solution.py:318
  57.9 0.0 collective-permute-done.received_ref
  57.9 0.0 copy-start.9
  57.9 0.8 copy-done.9
  58.7 0.0 copy-start.10
  58.7 1.0 %copy-done.10 = bf16[1024,256]{1,0:T(8,128)(2,1)S(1)} copy-done((bf16[1024,256]{1,0:T(8,128)(2,1)S(1)}, bf16[1024,256]{1,0:T(8,128)(2,1)}, u32[]{:S(2)}) %copy-start.10) | copy-done | bytes 524312
  59.8 0.1 join_weights.1.weight_ref
  59.9 12.6 %all-to-all-done.1.rows_ref = bf16[64,32,128]{2,1,0:T(8,128)(2,1)S(1)} async-done(((bf16[64,32,128]{2,1,0:T(8,128)(2,1)}), bf16[64,32,128]{2,1,0:T(8,128)(2,1)S(1)}, u32[]{:S(2)}, u32[]{:S(2)}) %all-to-all-start.1) | async-done | bytes 524320 | tf_op jit(solution)/shard_map/all_to_all | solution.py:318
  72.5 0.7 project.1
  73.2 17.6 %all_to_all.15.sums_ref = bf16[16,32,256]{2,1,0:T(8,128)(2,1)S(1)} all-to-all(bf16[16,32,256]{2,1,0:T(8,128)(2,1)S(1)} %bitcast.10), channel_id=1, replica_groups=mesh['y'=8,'zh'=4,'zp'=2,'tp'=8] {'zp','tp'}, dimensions={0} | all-to-all | bytes 524288 | tf_op jit(solution)/shard_map/all_to_all | solution.py:337
  90.8 0.6 finish.1
  (1 shorter events, 0.0 us)
Async XLA Ops:
  2.3 20.6 %copy-start = (bf16[64,64,128]{2,1,0:T(8,128)(2,1)S(1)}, bf16[64,64,128]{2,1,0:T(8,128)(2,1)}, u32[]{:S(2)}) copy-start(bf16[64,64,128]{2,1,0:T(8,128)(2,1)} %pack_lent.1.packed_ref) | copy-start | bytes 3145732
  2.3 20.6 %copy-start.1 = (bf16[2048,256]{1,0:T(8,128)(2,1)S(1)}, bf16[2048,256]{1,0:T(8,128)(2,1)}, u32[]{:S(2)}) copy-start(bf16[2048,256]{1,0:T(8,128)(2,1)} %mine_ref.1) | copy-start | bytes 3145732
  2.3 42.2 %all-to-all-start = ((bf16[64,64,128]{2,1,0:T(8,128)(2,1)}), bf16[64,64,128]{2,1,0:T(8,128)(2,1)S(1)}, u32[]{:S(2)}, u32[]{:S(2)}) async-start(bf16[64,64,128]{2,1,0:T(8,128)(2,1)} %pack_lent.1.packed_ref), calls=%async_computation | async-start | bytes 2097152 | tf_op jit(solution)/shard_map/all_to_all | solution.py:267
  22.1 0.7 copy-start.11
  22.8 0.7 copy-start.4
  23.5 3.3 %copy-start.2 = (bf16[4,256,1,128]{3,1,2,0:T(8,128)(2,1)S(1)}, bf16[4,256,1,128]{3,1,2,0:T(8,128)(2,1)}, u32[]{:S(2)}) copy-start(bf16[4,256,1,128]{3,1,2,0:T(8,128)(2,1)} %param.15) | copy-start | bytes 786436
  23.5 3.3 %copy-start.3 = (bf16[4,256,1,128]{3,1,2,0:T(8,128)(2,1)S(1)}, bf16[4,256,1,128]{3,1,2,0:T(8,128)(2,1)}, u32[]{:S(2)}) copy-start(bf16[4,256,1,128]{3,1,2,0:T(8,128)(2,1)} %param.16) | copy-start | bytes 786436
  23.5 3.3 %copy-start.5 = (bf16[32,256]{1,0:T(8,128)(2,1)S(1)}, bf16[32,256]{1,0:T(8,128)(2,1)}, u32[]{:S(2)}) copy-start(bf16[32,256]{1,0:T(8,128)(2,1)} %residual_ref.1) | copy-start | bytes 49156
  23.5 3.3 %copy-start.7 = (bf16[4,1,128]{2,0,1:T(4,128)(2,1)S(1)}, bf16[4,1,128]{2,0,1:T(4,128)(2,1)}, u32[]{:S(2)}) copy-start(bf16[4,1,128]{2,0,1:T(4,128)(2,1)} %param.14) | copy-start | bytes 3076
  24.6 33.3 %collective-permute-start = (bf16[1024,256]{1,0:T(8,128)(2,1)}, bf16[1024,256]{1,0:T(8,128)(2,1)S(1)}, u32[]{:S(2)}, u32[]{:S(2)}) collective-permute-start(bf16[1024,256]{1,0:T(8,128)(2,1)} %get-tuple-element.15), channel_id=1, source_target_pairs={{0,8},{8,0},{1,9},{9,1},{2,10},{10,2},{3,11},{11,3},{4,12},{12,4},... | collective-permute-start | bytes 1572872 | tf_op jit(solution)/shard_map/ppermute | solution.py:288
  26.8 0.7 copy-start.6
  26.8 0.7 copy-start.8
  47.7 24.7 %all-to-all-start.1 = ((bf16[64,32,128]{2,1,0:T(8,128)(2,1)}), bf16[64,32,128]{2,1,0:T(8,128)(2,1)S(1)}, u32[]{:S(2)}, u32[]{:S(2)}) async-start(bf16[64,32,128]{2,1,0:T(8,128)(2,1)} %attend.1), calls=%async_computation.1 | async-start | bytes 1048576 | tf_op jit(solution)/shard_map/all_to_all | solution.py:318
  57.9 0.8 copy-start.9
  58.7 1.0 %copy-start.10 = (bf16[1024,256]{1,0:T(8,128)(2,1)S(1)}, bf16[1024,256]{1,0:T(8,128)(2,1)}, u32[]{:S(2)}) copy-start(bf16[1024,256]{1,0:T(8,128)(2,1)} %copy-done.9) | copy-start | bytes 1572868

commit v2 on v1

--- a/solution.py
+++ b/solution.py
@@ -65,7 +65,8 @@
             picked = jnp.where(s == 1.0, query[1], query[0])
             picked = jnp.where(s == 2.0, query[2], picked)
             rows.append(jnp.where(s == 3.0, query[3], picked))
-        asked_ref[g] = jnp.concatenate(rows, axis=0).T.astype(BF16)
+        asked_ref[g, :128] = jnp.concatenate(rows, axis=0).astype(BF16)
+        asked_ref[g, 128:] = (iota((16, 128), 1) == 0).astype(F32).astype(BF16)
     group = iota((8, 128), 1) >> 4
     split = source.reshape(8, 8, 128)
     req = jnp.zeros((8, 128), F32)
@@ -136,29 +137,23 @@
 
 
 def attend_kernel(q_ref, req_ref, stat_ref, home_ref, recv_ref, out_ref, mixed_ref):
-    owner = iota((32, 128), 1) >> 4
-    far_tops, far_totals = [], []
+    block = (iota((128, 256), 0) >> 4) == (iota((128, 256), 1) >> 5)
+    lane = iota((128, 128), 1)
+    columns = jnp.zeros((128, 128), F32)
     for g in range(8):
-        here = pl.ds(8 * g, 8)
-        keys = recv_ref[here, :32, :].reshape(256, 128)
-        raw = dot(keys, q_ref[g], NN)
-        mark = keys.astype(F32)
-        scores, marks = raw[:32], mark[:32]
-        for j in range(1, 8):
-            scores = jnp.where(owner == j, raw[32 * j : 32 * j + 32], scores)
-            marks = jnp.where(owner == j, mark[32 * j : 32 * j + 32], marks)
-        scores = jnp.where(marks < 0.5 * ABSENT, scores * SCALE, VERY_LOW)
-        top = jnp.max(scores, axis=0, keepdims=True)
+        group = pl.ds(8 * g, 8)
+        keys = recv_ref[group, :32, :].reshape(256, 128)
+        raw = dot(q_ref[g], keys, NT)
+        valid = block & (raw[128:129] < 0.5 * ABSENT)
+        scores = jnp.where(valid, raw[:128] * SCALE, VERY_LOW)
+        top = jnp.max(scores, axis=1, keepdims=True)
         weights = jnp.exp(scores - top)
-        far_tops.append(top)
-        far_totals.append(jnp.sum(weights, axis=0, keepdims=True))
-        blocks = jnp.concatenate(
-            [jnp.where(owner == j, weights, 0.0) for j in range(8)], axis=0
-        ).astype(BF16)
-        values = recv_ref[here, 32:, :].reshape(256, 128)
-        mixed_ref[128 * g : 128 * g + 128] = dot(blocks, values, TN)
-    far_top = jnp.concatenate(far_tops, axis=0)
-    far_total = jnp.concatenate(far_totals, axis=0)
+        total = jnp.sum(weights, axis=1, keepdims=True)
+        columns = jnp.where(lane == g, top, jnp.where(lane == 8 + g, total, columns))
+        values = recv_ref[group, 32:, :].reshape(256, 128)
+        mixed_ref[128 * g : 128 * g + 128] = dot(weights.astype(BF16), values, NN)
+    stats = columns.T
+    far_top, far_total = stats[:8], stats[8:16]
     near_top, near_total = stat_ref[0:1], stat_ref[1:2]
     which = iota((1, 128), 1) >> 4
     req = req_ref[...]
@@ -213,7 +208,8 @@
     move = p == 32 * ((q >> 2) & 7) + 8 * (q & 3) + (q >> 5)
     move = move.astype(F32).astype(BF16)
     for b in range(8):
-        moved = dot(move, rows_ref[8 * b : 8 * b + 8].reshape(256, 128), NN).astype(BF16)
+        parts = [rows_ref[(8 * b + i - FIRST) % 64] for i in range(8)]
+        moved = dot(move, jnp.concatenate(parts, axis=0), NN).astype(BF16)
         for h in range(8):
             wide_ref[32 * b : 32 * b + 32, 128 * h : 128 * h + 128] = moved[32 * h : 32 * h + 32]
     wide = wide_ref[...]
@@ -270,7 +266,7 @@
     asked, req, sent = pl.pallas_call(
         ask_kernel,
         out_shape=(
-            jax.ShapeDtypeStruct((8, 128, 128), BF16),
+            jax.ShapeDtypeStruct((8, 144, 128), BF16),
             jax.ShapeDtypeStruct((8, 128), F32),
             jax.ShapeDtypeStruct((1024, 256), BF16),
         ),
@@ -315,7 +311,9 @@
         compiler_params=PARAMS,
         name="attend",
     )(asked, req, home_stat, home_out, recv)
-    rows = lax.all_to_all(copies, INST, split_axis=0, concat_axis=0, tiled=True)
+    rows = lax.all_to_all(
+        copies, INST, split_axis=0, concat_axis=0, tiled=True, axis_index_groups=ORDER
+    )
     weights = pl.pallas_call(
         join_kernel,
         out_shape=jax.ShapeDtypeStruct((2, 1024, 256), BF16),

time: 92.2 us -> 90.7 us (0.984)
  starting transfers between devices: 32.2 us -> 35.6 us
  waiting for transfers between devices: 28.5 us -> 25.6 us
  blocking collectives: 17.6 us -> 15.3 us
    all_to_all x1, starting transfers between devices: 10.2 us -> 13.6 us  [body(): lax.all_to_all(copies, INST, split_axis=0, concat_axis=0, tiled=True, axi...]
    all_to_all x1, waiting for transfers between devices: 12.6 us -> 9.59 us  [body(): lax.all_to_all(copies, INST, split_axis=0, concat_axis=0, tiled=True, axi...]
    all_to_all x1, blocking collectives: 17.6 us -> 15.3 us  [body(): lax.all_to_all(partial.reshape(16, 32, 256), ('zp', 'tp'), split_axis=0,...]
where the time goes in v2:
time: 90.7 us; the launch traced here: 90 us
  starting transfers between devices  35.6 us (39%)
  waiting for transfers between devices  25.6 us (28%)
  blocking collectives  15.3 us (17%)
  Pallas kernels  9.44 us (10%)
  local copies, waits for them, and re-layouts  3.89 us (4%)
    all_to_all x1, starting transfers between devices, body(): lax.all_to_all(packed, INST, split_axis=0, concat_axis=0, tiled=True, axi...  19.8 us
    all_to_all x1, waiting for transfers between devices, body(): lax.all_to_all(packed, INST, split_axis=0, concat_axis=0, tiled=True, axi...  16 us
    all_to_all x1, blocking collectives, body(): lax.all_to_all(partial.reshape(16, 32, 256), ('zp', 'tp'), split_axis=0,...  15.3 us
    all_to_all x1, starting transfers between devices, body(): lax.all_to_all(copies, INST, split_axis=0, concat_axis=0, tiled=True, axi...  13.6 us
    all_to_all x1, waiting for transfers between devices, body(): lax.all_to_all(copies, INST, split_axis=0, concat_axis=0, tiled=True, axi...  9.59 us
    unnamed x24, local copies, waits for them, and re-layouts  3.89 us
    pallas_call x1, Pallas kernels, body(): pl.pallas_call(attend_kernel, out_shape=jax.ShapeDtypeStruct((64, 32, 128...  3.76 us
    pallas_call x1, Pallas kernels, body(): pl.pallas_call(pack_kernel, out_shape=jax.ShapeDtypeStruct((64, 64, 128),...  2.24 us
  transfers between devices with their start and end apart: 3, of which 2 were waited for; matrix products, arithmetic and copies ran while one was open for 0% of the time, Pallas kernels for 6%

profile of v2, /device:TPU:1, one launch (start us, length us, event | category | flops | bytes accessed | tf_op | source)
XLA Modules:
  0.0 90.0 jit_solution(6729887235459411792)
XLA Ops:
  0.0 2.2 %pack_lent.1.packed_ref = bf16[64,64,128]{2,1,0:T(8,128)(2,1)} custom-call(s32[4032]{0:T(1024)} %req_ref.1, s32[63]{0:T(128)} %len_ref.2, bf16[63,32,128]{2,1,0:T(8,128)(2,1)} %bitcast.15, bf16[63,32,128]{2,1,0:T(8,128)(2,1)} %bitcast.16), custom_call_target="tpu_custom_call" | custom-call | tf_op jit(solution)/shard_map/pack_lent/pallas_call | solution.py:242
  2.3 0.0 copy-start
  2.3 0.0 copy-start.1
  2.3 19.8 %all-to-all-start = ((bf16[64,64,128]{2,1,0:T(8,128)(2,1)}), bf16[64,64,128]{2,1,0:T(8,128)(2,1)S(1)}, u32[]{:S(2)}, u32[]{:S(2)}) async-start(bf16[64,64,128]{2,1,0:T(8,128)(2,1)} %pack_lent.1.packed_ref), calls=%async_computation | async-start | bytes 2097152 | tf_op jit(solution)/shard_map/all_to_all | solution.py:263
  22.1 0.0 copy-start.11
  22.1 0.7 copy-done.11
  22.8 0.0 copy-start.4
  22.8 0.0 copy-done
  22.8 0.0 copy-done.1
  22.8 0.7 copy-done.4
  23.5 0.0 copy-start.2
  23.5 0.0 copy-start.3
  23.5 0.0 copy-start.5
  23.5 0.0 copy-start.7
  23.5 0.9 %ask_queries.1 = (bf16[8,144,128]{2,1,0:T(8,128)(2,1)S(1)}, f32[8,128]{1,0:T(8,128)S(1)}, bf16[1024,256]{1,0:T(8,128)(2,1)}) custom-call(s32[1]{0:T(128)} %bitcast.here_ref, s32[32,128]{1,0:T(8,128)S(1)} %pad_bitcast_fusion.table_ref, bf16[4,16,128]{2,1,0:T(8,128)(2,1)S(1)} %copy-done.4, bf16[2048,256]{1,0:T(8,128)(2,1)S(1)} %copy-done.1, ...), custom_call_target="tpu_custom_call" | custom-call | tf_op jit(solution)/shard_map/ask_queries/pallas_call | solution.py:266
  24.5 2.2 %collective-permute-start = (bf16[1024,256]{1,0:T(8,128)(2,1)}, bf16[1024,256]{1,0:T(8,128)(2,1)S(1)}, u32[]{:S(2)}, u32[]{:S(2)}) collective-permute-start(bf16[1024,256]{1,0:T(8,128)(2,1)} %get-tuple-element.15), channel_id=1, source_target_pairs={{0,8},{8,0},{1,9},{9,1},{2,10},{10,2},{3,11},{11,3},{4,12},{12,4},... | collective-permute-start | bytes 1572872 | tf_op jit(solution)/shard_map/ppermute | solution.py:284
  26.7 0.0 copy-start.6
  26.7 0.0 copy-start.8
  26.7 0.0 copy-done.2
  26.7 0.0 copy-done.3
  26.7 0.0 copy-done.5
  26.7 0.0 copy-done.7
  26.7 0.6 copy-done.6
  27.3 0.0 copy-done.8
  27.3 1.1 %home_part.1 = (f32[64,128]{1,0:T(8,128)S(1)}, f32[2,128]{1,0:T(2,128)S(1)}, f32[32,256]{1,0:T(8,128)S(1)}) custom-call(s32[4]{0:T(128)S(1)} %copy-done.8, bf16[4,16,128]{2,1,0:T(8,128)(2,1)S(1)} %copy-done.4, bf16[4,128]{1,0:T(4,128)(2,1)S(1)} %bitcast.13, bf16[4,128]{1,0:T(4,128)(2,1)S(1)} %bitcast.14, bf16[4,256,128]{2,1,0:T(8,128)(2,1)S(1)} %bitcast.11, ...), custom_call_target="tpu_custom_call" | custom-call | tf_op jit(solution)/shard_map/home_part/pallas_call | solution.py:285
  28.4 16.0 %all-to-all-done.recv_ref = bf16[64,64,128]{2,1,0:T(8,128)(2,1)S(1)} async-done(((bf16[64,64,128]{2,1,0:T(8,128)(2,1)}), bf16[64,64,128]{2,1,0:T(8,128)(2,1)S(1)}, u32[]{:S(2)}, u32[]{:S(2)}) %all-to-all-start) | async-done | bytes 1048608 | tf_op jit(solution)/shard_map/all_to_all | solution.py:263
  44.4 3.8 %attend.1 = bf16[64,32,128]{2,1,0:T(8,128)(2,1)} custom-call(bf16[8,144,128]{2,1,0:T(8,128)(2,1)S(1)} %get-tuple-element.11.q_ref, f32[8,128]{1,0:T(8,128)S(1)} %get-tuple-element.12.req_ref, f32[2,128]{1,0:T(2,128)S(1)} %get-tuple-element.13.stat_ref, f32[64,128]{1,0:T(8,128)S(1)} %get-tuple-element.14.home_ref, bf16[64,64,128]{2,1,0:T(8,128)(2,1)S(1)} %all-to-all-done.recv_ref), custom_call_target="tpu_custom_call" | custom-call | tf_op jit(solution)/shard_map/attend/pallas_call | solution.py:305
  48.2 13.6 %all-to-all-start.1 = ((bf16[64,32,128]{2,1,0:T(8,128)(2,1)}), bf16[64,32,128]{2,1,0:T(8,128)(2,1)S(1)}, u32[]{:S(2)}, u32[]{:S(2)}) async-start(bf16[64,32,128]{2,1,0:T(8,128)(2,1)} %attend.1), calls=%async_computation.1 | async-start | bytes 1048576 | tf_op jit(solution)/shard_map/all_to_all | solution.py:314
  61.8 0.0 collective-permute-done.received_ref
  61.8 0.0 copy-start.9
  61.8 0.8 copy-done.9
  62.6 0.0 copy-start.10
  62.6 1.0 %copy-done.10 = bf16[1024,256]{1,0:T(8,128)(2,1)S(1)} copy-done((bf16[1024,256]{1,0:T(8,128)(2,1)S(1)}, bf16[1024,256]{1,0:T(8,128)(2,1)}, u32[]{:S(2)}) %copy-start.10) | copy-done | bytes 524312
  63.7 0.1 join_weights.1.weight_ref
  63.7 9.6 %all-to-all-done.1.rows_ref = bf16[64,32,128]{2,1,0:T(8,128)(2,1)S(1)} async-done(((bf16[64,32,128]{2,1,0:T(8,128)(2,1)}), bf16[64,32,128]{2,1,0:T(8,128)(2,1)S(1)}, u32[]{:S(2)}, u32[]{:S(2)}) %all-to-all-start.1) | async-done | bytes 524320 | tf_op jit(solution)/shard_map/all_to_all | solution.py:314
  73.3 0.7 project.1
  74.1 15.3 %all_to_all.15.sums_ref = bf16[16,32,256]{2,1,0:T(8,128)(2,1)S(1)} all-to-all(bf16[16,32,256]{2,1,0:T(8,128)(2,1)S(1)} %bitcast.10), channel_id=1, replica_groups=mesh['y'=8,'zh'=4,'zp'=2,'tp'=8] {'zp','tp'}, dimensions={0} | all-to-all | bytes 524288 | tf_op jit(solution)/shard_map/all_to_all | solution.py:335
  89.4 0.6 finish.1
  (1 shorter events, 0.0 us)
Async XLA Ops:
  2.3 20.6 %copy-start = (bf16[64,64,128]{2,1,0:T(8,128)(2,1)S(1)}, bf16[64,64,128]{2,1,0:T(8,128)(2,1)}, u32[]{:S(2)}) copy-start(bf16[64,64,128]{2,1,0:T(8,128)(2,1)} %pack_lent.1.packed_ref) | copy-start | bytes 3145732
  2.3 20.6 %copy-start.1 = (bf16[2048,256]{1,0:T(8,128)(2,1)S(1)}, bf16[2048,256]{1,0:T(8,128)(2,1)}, u32[]{:S(2)}) copy-start(bf16[2048,256]{1,0:T(8,128)(2,1)} %mine_ref.1) | copy-start | bytes 3145732
  2.3 42.2 %all-to-all-start = ((bf16[64,64,128]{2,1,0:T(8,128)(2,1)}), bf16[64,64,128]{2,1,0:T(8,128)(2,1)S(1)}, u32[]{:S(2)}, u32[]{:S(2)}) async-start(bf16[64,64,128]{2,1,0:T(8,128)(2,1)} %pack_lent.1.packed_ref), calls=%async_computation | async-start | bytes 2097152 | tf_op jit(solution)/shard_map/all_to_all | solution.py:263
  22.1 0.7 copy-start.11
  22.8 0.7 copy-start.4
  23.5 3.1 %copy-start.2 = (bf16[4,256,1,128]{3,1,2,0:T(8,128)(2,1)S(1)}, bf16[4,256,1,128]{3,1,2,0:T(8,128)(2,1)}, u32[]{:S(2)}) copy-start(bf16[4,256,1,128]{3,1,2,0:T(8,128)(2,1)} %param.15) | copy-start | bytes 786436
  23.5 3.2 %copy-start.3 = (bf16[4,256,1,128]{3,1,2,0:T(8,128)(2,1)S(1)}, bf16[4,256,1,128]{3,1,2,0:T(8,128)(2,1)}, u32[]{:S(2)}) copy-start(bf16[4,256,1,128]{3,1,2,0:T(8,128)(2,1)} %param.16) | copy-start | bytes 786436
  23.5 3.2 %copy-start.5 = (bf16[32,256]{1,0:T(8,128)(2,1)S(1)}, bf16[32,256]{1,0:T(8,128)(2,1)}, u32[]{:S(2)}) copy-start(bf16[32,256]{1,0:T(8,128)(2,1)} %residual_ref.1) | copy-start | bytes 49156
  23.5 3.2 %copy-start.7 = (bf16[4,1,128]{2,0,1:T(4,128)(2,1)S(1)}, bf16[4,1,128]{2,0,1:T(4,128)(2,1)}, u32[]{:S(2)}) copy-start(bf16[4,1,128]{2,0,1:T(4,128)(2,1)} %param.14) | copy-start | bytes 3076
  24.5 37.3 %collective-permute-start = (bf16[1024,256]{1,0:T(8,128)(2,1)}, bf16[1024,256]{1,0:T(8,128)(2,1)S(1)}, u32[]{:S(2)}, u32[]{:S(2)}) collective-permute-start(bf16[1024,256]{1,0:T(8,128)(2,1)} %get-tuple-element.15), channel_id=1, source_target_pairs={{0,8},{8,0},{1,9},{9,1},{2,10},{10,2},{3,11},{11,3},{4,12},{12,4},... | collective-permute-start | bytes 1572872 | tf_op jit(solution)/shard_map/ppermute | solution.py:284
  26.7 0.7 copy-start.6
  26.7 0.7 copy-start.8
  48.2 25.2 %all-to-all-start.1 = ((bf16[64,32,128]{2,1,0:T(8,128)(2,1)}), bf16[64,32,128]{2,1,0:T(8,128)(2,1)S(1)}, u32[]{:S(2)}, u32[]{:S(2)}) async-start(bf16[64,32,128]{2,1,0:T(8,128)(2,1)} %attend.1), calls=%async_computation.1 | async-start | bytes 1048576 | tf_op jit(solution)/shard_map/all_to_all | solution.py:314
  61.8 0.8 copy-start.9
  62.6 1.0 %copy-start.10 = (bf16[1024,256]{1,0:T(8,128)(2,1)S(1)}, bf16[1024,256]{1,0:T(8,128)(2,1)}, u32[]{:S(2)}) copy-start(bf16[1024,256]{1,0:T(8,128)(2,1)} %copy-done.9) | copy-start | bytes 1572868

commit v3 on v1

--- a/solution.py
+++ b/solution.py
@@ -94,7 +94,9 @@
     for load in loads[:3]:
         load.wait()
     for s in range(63):
-        keys = jnp.where(token < len_in[s], k_in[s].astype(F32), ABSENT)
+        length = len_in[s]
+        absent = ABSENT + length.astype(F32)
+        keys = jnp.where(token < length, k_in[s].astype(F32), absent)
         keys_ref[((req_in[63 * here + s] >> 2) - FIRST) & 63] = keys.astype(BF16)
     send_keys = pltpu.make_async_copy(keys_ref, out_ref.at[:, pl.ds(0, 32)], sems.at[4])
     send_keys.start()
@@ -137,25 +139,28 @@
 
 def attend_kernel(q_ref, req_ref, stat_ref, home_ref, recv_ref, out_ref, mixed_ref):
     owner = iota((32, 128), 1) >> 4
+    token = iota((32, 128), 0).astype(F32)
+    holder = (iota((8, 128), 1) >> 4) == iota((8, 128), 0)
+    keep = [(owner == j).astype(F32).astype(BF16) for j in range(8)]
     far_tops, far_totals = [], []
     for g in range(8):
-        here = pl.ds(8 * g, 8)
-        keys = recv_ref[here, :32, :].reshape(256, 128)
+        group = pl.ds(8 * g, 8)
+        keys = recv_ref[group, :32, :].reshape(256, 128)
         raw = dot(keys, q_ref[g], NN)
-        mark = keys.astype(F32)
-        scores, marks = raw[:32], mark[:32]
+        last = recv_ref[group, 31, :].astype(F32)
+        length = jnp.where(last < 0.5 * ABSENT, 32.0, last - ABSENT)
+        length = jnp.sum(jnp.where(holder, length, 0.0), axis=0, keepdims=True)
+        scores = raw[:32]
         for j in range(1, 8):
             scores = jnp.where(owner == j, raw[32 * j : 32 * j + 32], scores)
-            marks = jnp.where(owner == j, mark[32 * j : 32 * j + 32], marks)
-        scores = jnp.where(marks < 0.5 * ABSENT, scores * SCALE, VERY_LOW)
+        scores = jnp.where(token < length, scores * SCALE, VERY_LOW)
         top = jnp.max(scores, axis=0, keepdims=True)
         weights = jnp.exp(scores - top)
         far_tops.append(top)
         far_totals.append(jnp.sum(weights, axis=0, keepdims=True))
-        blocks = jnp.concatenate(
-            [jnp.where(owner == j, weights, 0.0) for j in range(8)], axis=0
-        ).astype(BF16)
-        values = recv_ref[here, 32:, :].reshape(256, 128)
+        weights = weights.astype(BF16)
+        blocks = jnp.concatenate([weights * keep[j] for j in range(8)], axis=0)
+        values = recv_ref[group, 32:, :].reshape(256, 128)
         mixed_ref[128 * g : 128 * g + 128] = dot(blocks, values, TN)
     far_top = jnp.concatenate(far_tops, axis=0)
     far_total = jnp.concatenate(far_totals, axis=0)
@@ -213,7 +218,8 @@
     move = p == 32 * ((q >> 2) & 7) + 8 * (q & 3) + (q >> 5)
     move = move.astype(F32).astype(BF16)
     for b in range(8):
-        moved = dot(move, rows_ref[8 * b : 8 * b + 8].reshape(256, 128), NN).astype(BF16)
+        parts = [rows_ref[(8 * b + i - FIRST) % 64] for i in range(8)]
+        moved = dot(move, jnp.concatenate(parts, axis=0), NN).astype(BF16)
         for h in range(8):
             wide_ref[32 * b : 32 * b + 32, 128 * h : 128 * h + 128] = moved[32 * h : 32 * h + 32]
     wide = wide_ref[...]
@@ -315,7 +321,9 @@
         compiler_params=PARAMS,
         name="attend",
     )(asked, req, home_stat, home_out, recv)
-    rows = lax.all_to_all(copies, INST, split_axis=0, concat_axis=0, tiled=True)
+    rows = lax.all_to_all(
+        copies, INST, split_axis=0, concat_axis=0, tiled=True, axis_index_groups=ORDER
+    )
     weights = pl.pallas_call(
         join_kernel,
         out_shape=jax.ShapeDtypeStruct((2, 1024, 256), BF16),

time: 92.2 us -> 90.3 us (0.979)
  starting transfers between devices: 32.2 us -> 35.6 us
  waiting for transfers between devices: 28.5 us -> 25.5 us
  blocking collectives: 17.6 us -> 15.3 us
    all_to_all x1, starting transfers between devices: 10.2 us -> 13.6 us  [body(): lax.all_to_all(copies, INST, split_axis=0, concat_axis=0, tiled=True, axi...]
    all_to_all x1, waiting for transfers between devices: 12.6 us -> 9.59 us  [body(): lax.all_to_all(copies, INST, split_axis=0, concat_axis=0, tiled=True, axi...]
    all_to_all x1, blocking collectives: 17.6 us -> 15.3 us  [body(): lax.all_to_all(partial.reshape(16, 32, 256), ('zp', 'tp'), split_axis=0,...]
where the time goes in v3:
time: 90.3 us; the launch traced here: 89.6 us
  starting transfers between devices  35.6 us (39%)
  waiting for transfers between devices  25.5 us (28%)
  blocking collectives  15.3 us (17%)
  Pallas kernels  9.17 us (10%)
  local copies, waits for them, and re-layouts  3.89 us (4%)
    all_to_all x1, starting transfers between devices, body(): lax.all_to_all(packed, INST, split_axis=0, concat_axis=0, tiled=True, axi...  19.8 us
    all_to_all x1, waiting for transfers between devices, body(): lax.all_to_all(packed, INST, split_axis=0, concat_axis=0, tiled=True, axi...  15.9 us
    all_to_all x1, blocking collectives, body(): lax.all_to_all(partial.reshape(16, 32, 256), ('zp', 'tp'), split_axis=0,...  15.3 us
    all_to_all x1, starting transfers between devices, body(): lax.all_to_all(copies, INST, split_axis=0, concat_axis=0, tiled=True, axi...  13.6 us
    all_to_all x1, waiting for transfers between devices, body(): lax.all_to_all(copies, INST, split_axis=0, concat_axis=0, tiled=True, axi...  9.59 us
    unnamed x24, local copies, waits for them, and re-layouts  3.89 us
    pallas_call x1, Pallas kernels, body(): pl.pallas_call(attend_kernel, out_shape=jax.ShapeDtypeStruct((64, 32, 128...  3.31 us
    pallas_call x1, Pallas kernels, body(): pl.pallas_call(pack_kernel, out_shape=jax.ShapeDtypeStruct((64, 64, 128),...  2.27 us
  transfers between devices with their start and end apart: 3, of which 2 were waited for; matrix products, arithmetic and copies ran while one was open for 0% of the time, Pallas kernels for 6%

profile of v3, /device:TPU:1, one launch (start us, length us, event | category | flops | bytes accessed | tf_op | source)
XLA Modules:
  0.0 89.6 jit_solution(8193119645455614166)
XLA Ops:
  0.0 2.3 %pack_lent.1.packed_ref = bf16[64,64,128]{2,1,0:T(8,128)(2,1)} custom-call(s32[4032]{0:T(1024)} %req_ref.1, s32[63]{0:T(128)} %len_ref.2, bf16[63,32,128]{2,1,0:T(8,128)(2,1)} %bitcast.15, bf16[63,32,128]{2,1,0:T(8,128)(2,1)} %bitcast.16), custom_call_target="tpu_custom_call" | custom-call | tf_op jit(solution)/shard_map/pack_lent/pallas_call | solution.py:252
  2.3 0.0 copy-start
  2.3 0.0 copy-start.1
  2.3 19.8 %all-to-all-start = ((bf16[64,64,128]{2,1,0:T(8,128)(2,1)}), bf16[64,64,128]{2,1,0:T(8,128)(2,1)S(1)}, u32[]{:S(2)}, u32[]{:S(2)}) async-start(bf16[64,64,128]{2,1,0:T(8,128)(2,1)} %pack_lent.1.packed_ref), calls=%async_computation | async-start | bytes 2097152 | tf_op jit(solution)/shard_map/all_to_all | solution.py:273
  22.1 0.0 copy-start.11
  22.1 0.7 copy-done.11
  22.8 0.0 copy-start.4
  22.9 0.0 copy-done
  22.9 0.0 copy-done.1
  22.9 0.7 copy-done.4
  23.6 0.0 copy-start.2
  23.6 0.0 copy-start.3
  23.6 0.0 copy-start.5
  23.6 0.0 copy-start.7
  23.6 1.1 %ask_queries.1 = (bf16[8,128,128]{2,1,0:T(8,128)(2,1)S(1)}, f32[8,128]{1,0:T(8,128)S(1)}, bf16[1024,256]{1,0:T(8,128)(2,1)}) custom-call(s32[1]{0:T(128)} %bitcast.here_ref, s32[32,128]{1,0:T(8,128)S(1)} %pad_bitcast_fusion.table_ref, bf16[4,16,128]{2,1,0:T(8,128)(2,1)S(1)} %copy-done.4, bf16[2048,256]{1,0:T(8,128)(2,1)S(1)} %copy-done.1, ...), custom_call_target="tpu_custom_call" | custom-call | tf_op jit(solution)/shard_map/ask_queries/pallas_call | solution.py:276
  24.6 2.2 %collective-permute-start = (bf16[1024,256]{1,0:T(8,128)(2,1)}, bf16[1024,256]{1,0:T(8,128)(2,1)S(1)}, u32[]{:S(2)}, u32[]{:S(2)}) collective-permute-start(bf16[1024,256]{1,0:T(8,128)(2,1)} %get-tuple-element.15), channel_id=1, source_target_pairs={{0,8},{8,0},{1,9},{9,1},{2,10},{10,2},{3,11},{11,3},{4,12},{12,4},... | collective-permute-start | bytes 1572872 | tf_op jit(solution)/shard_map/ppermute | solution.py:294
  26.8 0.0 copy-start.6
  26.9 0.0 copy-start.8
  26.9 0.0 copy-done.2
  26.9 0.0 copy-done.3
  26.9 0.0 copy-done.5
  26.9 0.0 copy-done.7
  26.9 0.6 copy-done.6
  27.5 0.0 copy-done.8
  27.5 1.1 %home_part.1 = (f32[64,128]{1,0:T(8,128)S(1)}, f32[2,128]{1,0:T(2,128)S(1)}, f32[32,256]{1,0:T(8,128)S(1)}) custom-call(s32[4]{0:T(128)S(1)} %copy-done.8, bf16[4,16,128]{2,1,0:T(8,128)(2,1)S(1)} %copy-done.4, bf16[4,128]{1,0:T(4,128)(2,1)S(1)} %bitcast.13, bf16[4,128]{1,0:T(4,128)(2,1)S(1)} %bitcast.14, bf16[4,256,128]{2,1,0:T(8,128)(2,1)S(1)} %bitcast.11, ...), custom_call_target="tpu_custom_call" | custom-call | tf_op jit(solution)/shard_map/home_part/pallas_call | solution.py:295
  28.6 15.9 %all-to-all-done.recv_ref = bf16[64,64,128]{2,1,0:T(8,128)(2,1)S(1)} async-done(((bf16[64,64,128]{2,1,0:T(8,128)(2,1)}), bf16[64,64,128]{2,1,0:T(8,128)(2,1)S(1)}, u32[]{:S(2)}, u32[]{:S(2)}) %all-to-all-start) | async-done | bytes 1048608 | tf_op jit(solution)/shard_map/all_to_all | solution.py:273
  44.5 3.3 %attend.1 = bf16[64,32,128]{2,1,0:T(8,128)(2,1)} custom-call(bf16[8,128,128]{2,1,0:T(8,128)(2,1)S(1)} %get-tuple-element.11.q_ref, f32[8,128]{1,0:T(8,128)S(1)} %get-tuple-element.12.req_ref, f32[2,128]{1,0:T(2,128)S(1)} %get-tuple-element.13.stat_ref, f32[64,128]{1,0:T(8,128)S(1)} %get-tuple-element.14.home_ref, bf16[64,64,128]{2,1,0:T(8,128)(2,1)S(1)} %all-to-all-done.recv_ref), custom_call_target="tpu_custom_call" | custom-call | tf_op jit(solution)/shard_map/attend/pallas_call | solution.py:315
  47.8 13.6 %all-to-all-start.1 = ((bf16[64,32,128]{2,1,0:T(8,128)(2,1)}), bf16[64,32,128]{2,1,0:T(8,128)(2,1)S(1)}, u32[]{:S(2)}, u32[]{:S(2)}) async-start(bf16[64,32,128]{2,1,0:T(8,128)(2,1)} %attend.1), calls=%async_computation.1 | async-start | bytes 1048576 | tf_op jit(solution)/shard_map/all_to_all | solution.py:324
  61.4 0.0 collective-permute-done.received_ref
  61.4 0.0 copy-start.9
  61.4 0.8 copy-done.9
  62.2 0.0 copy-start.10
  62.2 1.0 %copy-done.10 = bf16[1024,256]{1,0:T(8,128)(2,1)S(1)} copy-done((bf16[1024,256]{1,0:T(8,128)(2,1)S(1)}, bf16[1024,256]{1,0:T(8,128)(2,1)}, u32[]{:S(2)}) %copy-start.10) | copy-done | bytes 524312
  63.3 0.1 join_weights.1.weight_ref
  63.3 9.6 %all-to-all-done.1.rows_ref = bf16[64,32,128]{2,1,0:T(8,128)(2,1)S(1)} async-done(((bf16[64,32,128]{2,1,0:T(8,128)(2,1)}), bf16[64,32,128]{2,1,0:T(8,128)(2,1)S(1)}, u32[]{:S(2)}, u32[]{:S(2)}) %all-to-all-start.1) | async-done | bytes 524320 | tf_op jit(solution)/shard_map/all_to_all | solution.py:324
  72.9 0.7 project.1
  73.7 15.3 %all_to_all.15.sums_ref = bf16[16,32,256]{2,1,0:T(8,128)(2,1)S(1)} all-to-all(bf16[16,32,256]{2,1,0:T(8,128)(2,1)S(1)} %bitcast.10), channel_id=1, replica_groups=mesh['y'=8,'zh'=4,'zp'=2,'tp'=8] {'zp','tp'}, dimensions={0} | all-to-all | bytes 524288 | tf_op jit(solution)/shard_map/all_to_all | solution.py:345
  88.9 0.6 finish.1
  (1 shorter events, 0.0 us)
Async XLA Ops:
  2.3 20.6 %copy-start = (bf16[64,64,128]{2,1,0:T(8,128)(2,1)S(1)}, bf16[64,64,128]{2,1,0:T(8,128)(2,1)}, u32[]{:S(2)}) copy-start(bf16[64,64,128]{2,1,0:T(8,128)(2,1)} %pack_lent.1.packed_ref) | copy-start | bytes 3145732
  2.3 20.6 %copy-start.1 = (bf16[2048,256]{1,0:T(8,128)(2,1)S(1)}, bf16[2048,256]{1,0:T(8,128)(2,1)}, u32[]{:S(2)}) copy-start(bf16[2048,256]{1,0:T(8,128)(2,1)} %mine_ref.1) | copy-start | bytes 3145732
  2.3 42.2 %all-to-all-start = ((bf16[64,64,128]{2,1,0:T(8,128)(2,1)}), bf16[64,64,128]{2,1,0:T(8,128)(2,1)S(1)}, u32[]{:S(2)}, u32[]{:S(2)}) async-start(bf16[64,64,128]{2,1,0:T(8,128)(2,1)} %pack_lent.1.packed_ref), calls=%async_computation | async-start | bytes 2097152 | tf_op jit(solution)/shard_map/all_to_all | solution.py:273
  22.1 0.7 copy-start.11
  22.8 0.7 copy-start.4
  23.6 3.3 %copy-start.2 = (bf16[4,256,1,128]{3,1,2,0:T(8,128)(2,1)S(1)}, bf16[4,256,1,128]{3,1,2,0:T(8,128)(2,1)}, u32[]{:S(2)}) copy-start(bf16[4,256,1,128]{3,1,2,0:T(8,128)(2,1)} %param.15) | copy-start | bytes 786436
  23.6 3.3 %copy-start.3 = (bf16[4,256,1,128]{3,1,2,0:T(8,128)(2,1)S(1)}, bf16[4,256,1,128]{3,1,2,0:T(8,128)(2,1)}, u32[]{:S(2)}) copy-start(bf16[4,256,1,128]{3,1,2,0:T(8,128)(2,1)} %param.16) | copy-start | bytes 786436
  23.6 3.3 %copy-start.5 = (bf16[32,256]{1,0:T(8,128)(2,1)S(1)}, bf16[32,256]{1,0:T(8,128)(2,1)}, u32[]{:S(2)}) copy-start(bf16[32,256]{1,0:T(8,128)(2,1)} %residual_ref.1) | copy-start | bytes 49156
  23.6 3.3 %copy-start.7 = (bf16[4,1,128]{2,0,1:T(4,128)(2,1)S(1)}, bf16[4,1,128]{2,0,1:T(4,128)(2,1)}, u32[]{:S(2)}) copy-start(bf16[4,1,128]{2,0,1:T(4,128)(2,1)} %param.14) | copy-start | bytes 3076
  24.6 36.7 %collective-permute-start = (bf16[1024,256]{1,0:T(8,128)(2,1)}, bf16[1024,256]{1,0:T(8,128)(2,1)S(1)}, u32[]{:S(2)}, u32[]{:S(2)}) collective-permute-start(bf16[1024,256]{1,0:T(8,128)(2,1)} %get-tuple-element.15), channel_id=1, source_target_pairs={{0,8},{8,0},{1,9},{9,1},{2,10},{10,2},{3,11},{11,3},{4,12},{12,4},... | collective-permute-start | bytes 1572872 | tf_op jit(solution)/shard_map/ppermute | solution.py:294
  26.8 0.7 copy-start.6
  26.9 0.7 copy-start.8
  47.8 25.2 %all-to-all-start.1 = ((bf16[64,32,128]{2,1,0:T(8,128)(2,1)}), bf16[64,32,128]{2,1,0:T(8,128)(2,1)S(1)}, u32[]{:S(2)}, u32[]{:S(2)}) async-start(bf16[64,32,128]{2,1,0:T(8,128)(2,1)} %attend.1), calls=%async_computation.1 | async-start | bytes 1048576 | tf_op jit(solution)/shard_map/all_to_all | solution.py:324
  61.4 0.8 copy-start.9
  62.2 1.0 %copy-start.10 = (bf16[1024,256]{1,0:T(8,128)(2,1)S(1)}, bf16[1024,256]{1,0:T(8,128)(2,1)}, u32[]{:S(2)}) copy-start(bf16[1024,256]{1,0:T(8,128)(2,1)} %copy-done.9) | copy-start | bytes 1572868

commit v4 on v3

--- a/solution.py
+++ b/solution.py
@@ -137,33 +137,39 @@
     base_ref[...] = residual_ref[...].astype(F32)
 
 
-def attend_kernel(q_ref, req_ref, stat_ref, home_ref, recv_ref, out_ref, mixed_ref):
+def attend_kernel(
+    q_ref, req_ref, stat_ref, home_ref, recv_ref, out_ref, raw_ref, mixed_ref
+):
     owner = iota((32, 128), 1) >> 4
-    token = iota((32, 128), 0).astype(F32)
-    holder = (iota((8, 128), 1) >> 4) == iota((8, 128), 0)
+    token = iota((8, 32, 128), 1).astype(F32)
+    holder = (iota((8, 8, 128), 2) >> 4) == iota((8, 8, 128), 1)
     keep = [(owner == j).astype(F32).astype(BF16) for j in range(8)]
-    far_tops, far_totals = [], []
     for g in range(8):
-        group = pl.ds(8 * g, 8)
-        keys = recv_ref[group, :32, :].reshape(256, 128)
-        raw = dot(keys, q_ref[g], NN)
-        last = recv_ref[group, 31, :].astype(F32)
-        length = jnp.where(last < 0.5 * ABSENT, 32.0, last - ABSENT)
-        length = jnp.sum(jnp.where(holder, length, 0.0), axis=0, keepdims=True)
-        scores = raw[:32]
+        keys = recv_ref[8 * g : 8 * g + 8, :32, :].reshape(256, 128)
+        raw_ref[256 * g : 256 * g + 256] = dot(keys, q_ref[g], NN)
+    last = recv_ref[:, 31, :].astype(F32).reshape(8, 8, 128)
+    length = jnp.where(last < 0.5 * ABSENT, 32.0, last - ABSENT)
+    length = jnp.sum(jnp.where(holder, length, 0.0), axis=1, keepdims=True)
+    scores = []
+    for g in range(8):
+        picked = raw_ref[256 * g : 256 * g + 32]
         for j in range(1, 8):
-            scores = jnp.where(owner == j, raw[32 * j : 32 * j + 32], scores)
-        scores = jnp.where(token < length, scores * SCALE, VERY_LOW)
-        top = jnp.max(scores, axis=0, keepdims=True)
-        weights = jnp.exp(scores - top)
-        far_tops.append(top)
-        far_totals.append(jnp.sum(weights, axis=0, keepdims=True))
-        weights = weights.astype(BF16)
-        blocks = jnp.concatenate([weights * keep[j] for j in range(8)], axis=0)
-        values = recv_ref[group, 32:, :].reshape(256, 128)
-        mixed_ref[128 * g : 128 * g + 128] = dot(blocks, values, TN)
-    far_top = jnp.concatenate(far_tops, axis=0)
-    far_total = jnp.concatenate(far_totals, axis=0)
+            first = 256 * g + 32 * j
+            picked = jnp.where(owner == j, raw_ref[first : first + 32], picked)
+        scores.append(picked)
+    scores = jnp.concatenate(scores, axis=0).reshape(8, 32, 128)
+    scores = jnp.where(token < length, scores * SCALE, VERY_LOW)
+    far_top = jnp.max(scores, axis=1, keepdims=True)
+    weights = jnp.exp(scores - far_top)
+    far_total = jnp.sum(weights, axis=1, keepdims=True).reshape(8, 128)
+    far_top = far_top.reshape(8, 128)
+    weights = weights.astype(BF16)
+    for g in range(8):
+        blocks = jnp.concatenate([weights[g] * keep[j] for j in range(8)], axis=0)
+        values = recv_ref[8 * g : 8 * g + 8, 32:, :].reshape(256, 128)
+        high, low = halves(dot(blocks, values, TN))
+        mixed_ref[128 * g : 128 * g + 128] = high
+        mixed_ref[1024 + 128 * g : 1024 + 128 * g + 128] = low
     near_top, near_total = stat_ref[0:1], stat_ref[1:2]
     which = iota((1, 128), 1) >> 4
     req = req_ref[...]
@@ -196,10 +202,11 @@
     acc = dot(high[:, :64], home_high, NN) + dot(high[:, :64], home_low, NN)
     acc += dot(low[:, :64], home_high, NN)
     far_w = [far_w[r] * scale[r : r + 1] for r in range(4)]
-    for g in range(8):
-        high, low = spread_rows([far_w[r][g : g + 1] for r in range(4)])
-        mixed_high, mixed_low = halves(mixed_ref[128 * g : 128 * g + 128])
-        acc += dot(high, mixed_high, NN) + dot(high, mixed_low, NN) + dot(low, mixed_high, NN)
+    spread = [spread_rows([far_w[r][g : g + 1] for r in range(4)]) for g in range(8)]
+    high = jnp.concatenate([h for h, _ in spread], axis=1)
+    low = jnp.concatenate([l for _, l in spread], axis=1)
+    mixed_high, mixed_low = mixed_ref[:1024], mixed_ref[1024:]
+    acc += dot(high, mixed_high, NN) + dot(high, mixed_low, NN) + dot(low, mixed_high, NN)
     lower = jnp.concatenate([acc[16 * r : 16 * r + 8] for r in range(4)], axis=0)
     upper = jnp.concatenate([acc[16 * r + 8 : 16 * r + 16] for r in range(4)], axis=0)
     split = jnp.concatenate([lower, upper], axis=0).astype(BF16).reshape(1, 2, 32, 128)
@@ -317,7 +324,7 @@
         out_shape=jax.ShapeDtypeStruct((64, 32, 128), BF16),
         in_specs=[VMEM] * 5,
         out_specs=VMEM,
-        scratch_shapes=[pltpu.VMEM((1024, 128), F32)],
+        scratch_shapes=[pltpu.VMEM((2048, 128), F32), pltpu.VMEM((2048, 128), BF16)],
         compiler_params=PARAMS,
         name="attend",
     )(asked, req, home_stat, home_out, recv)

time: 90.3 us -> 88.9 us (0.984)
  Pallas kernels: 9.17 us -> 7.75 us
    pallas_call x1, Pallas kernels: 3.31 us -> 1.89 us  [body(): pl.pallas_call(attend_kernel, out_shape=jax.ShapeDtypeStruct((64, 32, 128...]
  transfers between devices with their start and end apart: 3 -> 3, of which waited for: 2 -> 2; matrix products, arithmetic and copies ran while one was open for 0% -> 0% of each run, Pallas kernels for 6% -> 5%
where the time goes in v4:
time: 88.9 us; the launch traced here: 88.2 us
  starting transfers between devices  35.6 us (40%)
  waiting for transfers between devices  25.5 us (29%)
  blocking collectives  15.3 us (17%)
  Pallas kernels  7.75 us (9%)
  local copies, waits for them, and re-layouts  3.89 us (4%)
    all_to_all x1, starting transfers between devices, body(): lax.all_to_all(packed, INST, split_axis=0, concat_axis=0, tiled=True, axi...  19.8 us
    all_to_all x1, waiting for transfers between devices, body(): lax.all_to_all(packed, INST, split_axis=0, concat_axis=0, tiled=True, axi...  15.9 us
    all_to_all x1, blocking collectives, body(): lax.all_to_all(partial.reshape(16, 32, 256), ('zp', 'tp'), split_axis=0,...  15.3 us
    all_to_all x1, starting transfers between devices, body(): lax.all_to_all(copies, INST, split_axis=0, concat_axis=0, tiled=True, axi...  13.6 us
    all_to_all x1, waiting for transfers between devices, body(): lax.all_to_all(copies, INST, split_axis=0, concat_axis=0, tiled=True, axi...  9.63 us
    unnamed x24, local copies, waits for them, and re-layouts  3.89 us
    pallas_call x1, Pallas kernels, body(): pl.pallas_call(pack_kernel, out_shape=jax.ShapeDtypeStruct((64, 64, 128),...  2.27 us
    ppermute x1, starting transfers between devices, body(): received = lax.ppermute(sent, 'zp', [(0, 1), (1, 0)])  2.18 us
  transfers between devices with their start and end apart: 3, of which 2 were waited for; matrix products, arithmetic and copies ran while one was open for 0% of the time, Pallas kernels for 5%

profile of v4, /device:TPU:1, one launch (start us, length us, event | category | flops | bytes accessed | tf_op | source)
XLA Modules:
  0.0 88.2 jit_solution(8893696925399154829)
XLA Ops:
  0.0 2.3 %pack_lent.1.packed_ref = bf16[64,64,128]{2,1,0:T(8,128)(2,1)} custom-call(s32[4032]{0:T(1024)} %req_ref.1, s32[63]{0:T(128)} %len_ref.2, bf16[63,32,128]{2,1,0:T(8,128)(2,1)} %bitcast.15, bf16[63,32,128]{2,1,0:T(8,128)(2,1)} %bitcast.16), custom_call_target="tpu_custom_call" | custom-call | tf_op jit(solution)/shard_map/pack_lent/pallas_call | solution.py:259
  2.3 0.0 copy-start
  2.3 0.0 copy-start.1
  2.3 19.8 %all-to-all-start = ((bf16[64,64,128]{2,1,0:T(8,128)(2,1)}), bf16[64,64,128]{2,1,0:T(8,128)(2,1)S(1)}, u32[]{:S(2)}, u32[]{:S(2)}) async-start(bf16[64,64,128]{2,1,0:T(8,128)(2,1)} %pack_lent.1.packed_ref), calls=%async_computation | async-start | bytes 2097152 | tf_op jit(solution)/shard_map/all_to_all | solution.py:280
  22.1 0.0 copy-start.11
  22.1 0.7 copy-done.11
  22.8 0.0 copy-start.4
  22.9 0.0 copy-done
  22.9 0.0 copy-done.1
  22.9 0.7 copy-done.4
  23.6 0.0 copy-start.2
  23.6 0.0 copy-start.3
  23.6 0.0 copy-start.5
  23.6 0.0 copy-start.7
  23.6 1.1 %ask_queries.1 = (bf16[8,128,128]{2,1,0:T(8,128)(2,1)S(1)}, f32[8,128]{1,0:T(8,128)S(1)}, bf16[1024,256]{1,0:T(8,128)(2,1)}) custom-call(s32[1]{0:T(128)} %bitcast.here_ref, s32[32,128]{1,0:T(8,128)S(1)} %pad_bitcast_fusion.table_ref, bf16[4,16,128]{2,1,0:T(8,128)(2,1)S(1)} %copy-done.4, bf16[2048,256]{1,0:T(8,128)(2,1)S(1)} %copy-done.1, ...), custom_call_target="tpu_custom_call" | custom-call | tf_op jit(solution)/shard_map/ask_queries/pallas_call | solution.py:283
  24.6 2.2 %collective-permute-start = (bf16[1024,256]{1,0:T(8,128)(2,1)}, bf16[1024,256]{1,0:T(8,128)(2,1)S(1)}, u32[]{:S(2)}, u32[]{:S(2)}) collective-permute-start(bf16[1024,256]{1,0:T(8,128)(2,1)} %get-tuple-element.15), channel_id=1, source_target_pairs={{0,8},{8,0},{1,9},{9,1},{2,10},{10,2},{3,11},{11,3},{4,12},{12,4},... | collective-permute-start | bytes 1572872 | tf_op jit(solution)/shard_map/ppermute | solution.py:301
  26.8 0.0 copy-start.6
  26.9 0.0 copy-start.8
  26.9 0.0 copy-done.2
  26.9 0.0 copy-done.3
  26.9 0.0 copy-done.5
  26.9 0.0 copy-done.7
  26.9 0.6 copy-done.6
  27.5 0.0 copy-done.8
  27.5 1.1 %home_part.1 = (f32[64,128]{1,0:T(8,128)S(1)}, f32[2,128]{1,0:T(2,128)S(1)}, f32[32,256]{1,0:T(8,128)S(1)}) custom-call(s32[4]{0:T(128)S(1)} %copy-done.8, bf16[4,16,128]{2,1,0:T(8,128)(2,1)S(1)} %copy-done.4, bf16[4,128]{1,0:T(4,128)(2,1)S(1)} %bitcast.13, bf16[4,128]{1,0:T(4,128)(2,1)S(1)} %bitcast.14, bf16[4,256,128]{2,1,0:T(8,128)(2,1)S(1)} %bitcast.11, ...), custom_call_target="tpu_custom_call" | custom-call | tf_op jit(solution)/shard_map/home_part/pallas_call | solution.py:302
  28.6 15.9 %all-to-all-done.recv_ref = bf16[64,64,128]{2,1,0:T(8,128)(2,1)S(1)} async-done(((bf16[64,64,128]{2,1,0:T(8,128)(2,1)}), bf16[64,64,128]{2,1,0:T(8,128)(2,1)S(1)}, u32[]{:S(2)}, u32[]{:S(2)}) %all-to-all-start) | async-done | bytes 1048608 | tf_op jit(solution)/shard_map/all_to_all | solution.py:280
  44.5 1.9 %attend.1 = bf16[64,32,128]{2,1,0:T(8,128)(2,1)} custom-call(bf16[8,128,128]{2,1,0:T(8,128)(2,1)S(1)} %get-tuple-element.11.q_ref, f32[8,128]{1,0:T(8,128)S(1)} %get-tuple-element.12.req_ref, f32[2,128]{1,0:T(2,128)S(1)} %get-tuple-element.13.stat_ref, f32[64,128]{1,0:T(8,128)S(1)} %get-tuple-element.14.home_ref, bf16[64,64,128]{2,1,0:T(8,128)(2,1)S(1)} %all-to-all-done.recv_ref), custom_call_target="tpu_custom_call" | custom-call | tf_op jit(solution)/shard_map/attend/pallas_call | solution.py:322
  46.4 13.6 %all-to-all-start.1 = ((bf16[64,32,128]{2,1,0:T(8,128)(2,1)}), bf16[64,32,128]{2,1,0:T(8,128)(2,1)S(1)}, u32[]{:S(2)}, u32[]{:S(2)}) async-start(bf16[64,32,128]{2,1,0:T(8,128)(2,1)} %attend.1), calls=%async_computation.1 | async-start | bytes 1048576 | tf_op jit(solution)/shard_map/all_to_all | solution.py:331
  60.0 0.0 collective-permute-done.received_ref
  60.0 0.0 copy-start.9
  60.0 0.8 copy-done.9
  60.8 0.0 copy-start.10
  60.8 1.0 %copy-done.10 = bf16[1024,256]{1,0:T(8,128)(2,1)S(1)} copy-done((bf16[1024,256]{1,0:T(8,128)(2,1)S(1)}, bf16[1024,256]{1,0:T(8,128)(2,1)}, u32[]{:S(2)}) %copy-start.10) | copy-done | bytes 524312
  61.8 0.1 join_weights.1.weight_ref
  61.9 9.6 %all-to-all-done.1.rows_ref = bf16[64,32,128]{2,1,0:T(8,128)(2,1)S(1)} async-done(((bf16[64,32,128]{2,1,0:T(8,128)(2,1)}), bf16[64,32,128]{2,1,0:T(8,128)(2,1)S(1)}, u32[]{:S(2)}, u32[]{:S(2)}) %all-to-all-start.1) | async-done | bytes 524320 | tf_op jit(solution)/shard_map/all_to_all | solution.py:331
  71.5 0.7 project.1
  72.3 15.3 %all_to_all.15.sums_ref = bf16[16,32,256]{2,1,0:T(8,128)(2,1)S(1)} all-to-all(bf16[16,32,256]{2,1,0:T(8,128)(2,1)S(1)} %bitcast.10), channel_id=1, replica_groups=mesh['y'=8,'zh'=4,'zp'=2,'tp'=8] {'zp','tp'}, dimensions={0} | all-to-all | bytes 524288 | tf_op jit(solution)/shard_map/all_to_all | solution.py:352
  87.5 0.6 finish.1
  (1 shorter events, 0.0 us)
Async XLA Ops:
  2.3 20.6 %copy-start = (bf16[64,64,128]{2,1,0:T(8,128)(2,1)S(1)}, bf16[64,64,128]{2,1,0:T(8,128)(2,1)}, u32[]{:S(2)}) copy-start(bf16[64,64,128]{2,1,0:T(8,128)(2,1)} %pack_lent.1.packed_ref) | copy-start | bytes 3145732
  2.3 20.6 %copy-start.1 = (bf16[2048,256]{1,0:T(8,128)(2,1)S(1)}, bf16[2048,256]{1,0:T(8,128)(2,1)}, u32[]{:S(2)}) copy-start(bf16[2048,256]{1,0:T(8,128)(2,1)} %mine_ref.1) | copy-start | bytes 3145732
  2.3 42.2 %all-to-all-start = ((bf16[64,64,128]{2,1,0:T(8,128)(2,1)}), bf16[64,64,128]{2,1,0:T(8,128)(2,1)S(1)}, u32[]{:S(2)}, u32[]{:S(2)}) async-start(bf16[64,64,128]{2,1,0:T(8,128)(2,1)} %pack_lent.1.packed_ref), calls=%async_computation | async-start | bytes 2097152 | tf_op jit(solution)/shard_map/all_to_all | solution.py:280
  22.1 0.7 copy-start.11
  22.8 0.7 copy-start.4
  23.6 3.3 %copy-start.2 = (bf16[4,256,1,128]{3,1,2,0:T(8,128)(2,1)S(1)}, bf16[4,256,1,128]{3,1,2,0:T(8,128)(2,1)}, u32[]{:S(2)}) copy-start(bf16[4,256,1,128]{3,1,2,0:T(8,128)(2,1)} %param.15) | copy-start | bytes 786436
  23.6 3.3 %copy-start.3 = (bf16[4,256,1,128]{3,1,2,0:T(8,128)(2,1)S(1)}, bf16[4,256,1,128]{3,1,2,0:T(8,128)(2,1)}, u32[]{:S(2)}) copy-start(bf16[4,256,1,128]{3,1,2,0:T(8,128)(2,1)} %param.16) | copy-start | bytes 786436
  23.6 3.3 %copy-start.5 = (bf16[32,256]{1,0:T(8,128)(2,1)S(1)}, bf16[32,256]{1,0:T(8,128)(2,1)}, u32[]{:S(2)}) copy-start(bf16[32,256]{1,0:T(8,128)(2,1)} %residual_ref.1) | copy-start | bytes 49156
  23.6 3.3 %copy-start.7 = (bf16[4,1,128]{2,0,1:T(4,128)(2,1)S(1)}, bf16[4,1,128]{2,0,1:T(4,128)(2,1)}, u32[]{:S(2)}) copy-start(bf16[4,1,128]{2,0,1:T(4,128)(2,1)} %param.14) | copy-start | bytes 3076
  24.6 35.3 %collective-permute-start = (bf16[1024,256]{1,0:T(8,128)(2,1)}, bf16[1024,256]{1,0:T(8,128)(2,1)S(1)}, u32[]{:S(2)}, u32[]{:S(2)}) collective-permute-start(bf16[1024,256]{1,0:T(8,128)(2,1)} %get-tuple-element.15), channel_id=1, source_target_pairs={{0,8},{8,0},{1,9},{9,1},{2,10},{10,2},{3,11},{11,3},{4,12},{12,4},... | collective-permute-start | bytes 1572872 | tf_op jit(solution)/shard_map/ppermute | solution.py:301
  26.8 0.7 copy-start.6
  26.9 0.7 copy-start.8
  46.4 25.2 %all-to-all-start.1 = ((bf16[64,32,128]{2,1,0:T(8,128)(2,1)}), bf16[64,32,128]{2,1,0:T(8,128)(2,1)S(1)}, u32[]{:S(2)}, u32[]{:S(2)}) async-start(bf16[64,32,128]{2,1,0:T(8,128)(2,1)} %attend.1), calls=%async_computation.1 | async-start | bytes 1048576 | tf_op jit(solution)/shard_map/all_to_all | solution.py:331
  60.0 0.8 copy-start.9
  60.8 1.0 %copy-start.10 = (bf16[1024,256]{1,0:T(8,128)(2,1)S(1)}, bf16[1024,256]{1,0:T(8,128)(2,1)}, u32[]{:S(2)}) copy-start(bf16[1024,256]{1,0:T(8,128)(2,1)} %copy-done.9) | copy-start | bytes 1572868

commit v5 on v4

--- a/solution.py
+++ b/solution.py
@@ -88,16 +88,15 @@
         load.start()
     here = lax.axis_index(INST)
     place = (here - FIRST) & 63
-    token = iota((32, 128), 0)
+    token = iota((32, 128), 0).astype(F32).astype(BF16)
     keys_ref[place] = jnp.full((32, 128), ABSENT, F32).astype(BF16)
     values_ref[place] = jnp.zeros((32, 128), F32).astype(BF16)
     for load in loads[:3]:
         load.wait()
     for s in range(63):
-        length = len_in[s]
-        absent = ABSENT + length.astype(F32)
-        keys = jnp.where(token < length, k_in[s].astype(F32), absent)
-        keys_ref[((req_in[63 * here + s] >> 2) - FIRST) & 63] = keys.astype(BF16)
+        length = jnp.full((32, 128), len_in[s].astype(F32), F32).astype(BF16)
+        keys = jnp.where(token < length, k_in[s], length + ABSENT)
+        keys_ref[((req_in[63 * here + s] >> 2) - FIRST) & 63] = keys
     send_keys = pltpu.make_async_copy(keys_ref, out_ref.at[:, pl.ds(0, 32)], sems.at[4])
     send_keys.start()
     loads[3].wait()

time: 88.9 us -> 88.9 us (level)
  no operation moved by 1% of the time
where the time goes in v5:
time: 88.9 us; the launch traced here: 88.2 us
  starting transfers between devices  35.6 us (40%)
  waiting for transfers between devices  25.5 us (29%)
  blocking collectives  15.3 us (17%)
  Pallas kernels  7.75 us (9%)
  local copies, waits for them, and re-layouts  3.89 us (4%)
    all_to_all x1, starting transfers between devices, body(): lax.all_to_all(packed, INST, split_axis=0, concat_axis=0, tiled=True, axi...  19.8 us
    all_to_all x1, waiting for transfers between devices, body(): lax.all_to_all(packed, INST, split_axis=0, concat_axis=0, tiled=True, axi...  15.9 us
    all_to_all x1, blocking collectives, body(): lax.all_to_all(partial.reshape(16, 32, 256), ('zp', 'tp'), split_axis=0,...  15.3 us
    all_to_all x1, starting transfers between devices, body(): lax.all_to_all(copies, INST, split_axis=0, concat_axis=0, tiled=True, axi...  13.6 us
    all_to_all x1, waiting for transfers between devices, body(): lax.all_to_all(copies, INST, split_axis=0, concat_axis=0, tiled=True, axi...  9.62 us
    unnamed x24, local copies, waits for them, and re-layouts  3.89 us
    pallas_call x1, Pallas kernels, body(): pl.pallas_call(pack_kernel, out_shape=jax.ShapeDtypeStruct((64, 64, 128),...  2.26 us
    ppermute x1, starting transfers between devices, body(): received = lax.ppermute(sent, 'zp', [(0, 1), (1, 0)])  2.18 us
  transfers between devices with their start and end apart: 3, of which 2 were waited for; matrix products, arithmetic and copies ran while one was open for 0% of the time, Pallas kernels for 5%

profile of v5, /device:TPU:1, one launch (start us, length us, event | category | flops | bytes accessed | tf_op | source)
XLA Modules:
  0.0 88.2 jit_solution(309472795735607875)
XLA Ops:
  0.0 2.3 %pack_lent.1.packed_ref = bf16[64,64,128]{2,1,0:T(8,128)(2,1)} custom-call(s32[4032]{0:T(1024)} %req_ref.1, s32[63]{0:T(128)} %len_ref.2, bf16[63,32,128]{2,1,0:T(8,128)(2,1)} %bitcast.15, bf16[63,32,128]{2,1,0:T(8,128)(2,1)} %bitcast.16), custom_call_target="tpu_custom_call" | custom-call | tf_op jit(solution)/shard_map/pack_lent/pallas_call | solution.py:258
  2.3 0.0 copy-start
  2.3 0.0 copy-start.1
  2.3 19.8 %all-to-all-start = ((bf16[64,64,128]{2,1,0:T(8,128)(2,1)}), bf16[64,64,128]{2,1,0:T(8,128)(2,1)S(1)}, u32[]{:S(2)}, u32[]{:S(2)}) async-start(bf16[64,64,128]{2,1,0:T(8,128)(2,1)} %pack_lent.1.packed_ref), calls=%async_computation | async-start | bytes 2097152 | tf_op jit(solution)/shard_map/all_to_all | solution.py:279
  22.1 0.0 copy-start.11
  22.1 0.7 copy-done.11
  22.8 0.0 copy-start.4
  22.8 0.0 copy-done
  22.8 0.0 copy-done.1
  22.9 0.7 copy-done.4
  23.6 0.0 copy-start.2
  23.6 0.0 copy-start.3
  23.6 0.0 copy-start.5
  23.6 0.0 copy-start.7
  23.6 1.1 %ask_queries.1 = (bf16[8,128,128]{2,1,0:T(8,128)(2,1)S(1)}, f32[8,128]{1,0:T(8,128)S(1)}, bf16[1024,256]{1,0:T(8,128)(2,1)}) custom-call(s32[1]{0:T(128)} %bitcast.here_ref, s32[32,128]{1,0:T(8,128)S(1)} %pad_bitcast_fusion.table_ref, bf16[4,16,128]{2,1,0:T(8,128)(2,1)S(1)} %copy-done.4, bf16[2048,256]{1,0:T(8,128)(2,1)S(1)} %copy-done.1, ...), custom_call_target="tpu_custom_call" | custom-call | tf_op jit(solution)/shard_map/ask_queries/pallas_call | solution.py:282
  24.6 2.2 %collective-permute-start = (bf16[1024,256]{1,0:T(8,128)(2,1)}, bf16[1024,256]{1,0:T(8,128)(2,1)S(1)}, u32[]{:S(2)}, u32[]{:S(2)}) collective-permute-start(bf16[1024,256]{1,0:T(8,128)(2,1)} %get-tuple-element.15), channel_id=1, source_target_pairs={{0,8},{8,0},{1,9},{9,1},{2,10},{10,2},{3,11},{11,3},{4,12},{12,4},... | collective-permute-start | bytes 1572872 | tf_op jit(solution)/shard_map/ppermute | solution.py:300
  26.8 0.0 copy-start.6
  26.8 0.0 copy-start.8
  26.9 0.0 copy-done.2
  26.9 0.0 copy-done.3
  26.9 0.0 copy-done.5
  26.9 0.0 copy-done.7
  26.9 0.6 copy-done.6
  27.5 0.0 copy-done.8
  27.5 1.1 %home_part.1 = (f32[64,128]{1,0:T(8,128)S(1)}, f32[2,128]{1,0:T(2,128)S(1)}, f32[32,256]{1,0:T(8,128)S(1)}) custom-call(s32[4]{0:T(128)S(1)} %copy-done.8, bf16[4,16,128]{2,1,0:T(8,128)(2,1)S(1)} %copy-done.4, bf16[4,128]{1,0:T(4,128)(2,1)S(1)} %bitcast.13, bf16[4,128]{1,0:T(4,128)(2,1)S(1)} %bitcast.14, bf16[4,256,128]{2,1,0:T(8,128)(2,1)S(1)} %bitcast.11, ...), custom_call_target="tpu_custom_call" | custom-call | tf_op jit(solution)/shard_map/home_part/pallas_call | solution.py:301
  28.6 15.9 %all-to-all-done.recv_ref = bf16[64,64,128]{2,1,0:T(8,128)(2,1)S(1)} async-done(((bf16[64,64,128]{2,1,0:T(8,128)(2,1)}), bf16[64,64,128]{2,1,0:T(8,128)(2,1)S(1)}, u32[]{:S(2)}, u32[]{:S(2)}) %all-to-all-start) | async-done | bytes 1048608 | tf_op jit(solution)/shard_map/all_to_all | solution.py:279
  44.4 1.9 %attend.1 = bf16[64,32,128]{2,1,0:T(8,128)(2,1)} custom-call(bf16[8,128,128]{2,1,0:T(8,128)(2,1)S(1)} %get-tuple-element.11.q_ref, f32[8,128]{1,0:T(8,128)S(1)} %get-tuple-element.12.req_ref, f32[2,128]{1,0:T(2,128)S(1)} %get-tuple-element.13.stat_ref, f32[64,128]{1,0:T(8,128)S(1)} %get-tuple-element.14.home_ref, bf16[64,64,128]{2,1,0:T(8,128)(2,1)S(1)} %all-to-all-done.recv_ref), custom_call_target="tpu_custom_call" | custom-call | tf_op jit(solution)/shard_map/attend/pallas_call | solution.py:321
  46.3 13.6 %all-to-all-start.1 = ((bf16[64,32,128]{2,1,0:T(8,128)(2,1)}), bf16[64,32,128]{2,1,0:T(8,128)(2,1)S(1)}, u32[]{:S(2)}, u32[]{:S(2)}) async-start(bf16[64,32,128]{2,1,0:T(8,128)(2,1)} %attend.1), calls=%async_computation.1 | async-start | bytes 1048576 | tf_op jit(solution)/shard_map/all_to_all | solution.py:330
  60.0 0.0 collective-permute-done.received_ref
  60.0 0.0 copy-start.9
  60.0 0.8 copy-done.9
  60.8 0.0 copy-start.10
  60.8 1.0 %copy-done.10 = bf16[1024,256]{1,0:T(8,128)(2,1)S(1)} copy-done((bf16[1024,256]{1,0:T(8,128)(2,1)S(1)}, bf16[1024,256]{1,0:T(8,128)(2,1)}, u32[]{:S(2)}) %copy-start.10) | copy-done | bytes 524312
  61.8 0.1 join_weights.1.weight_ref
  61.9 9.6 %all-to-all-done.1.rows_ref = bf16[64,32,128]{2,1,0:T(8,128)(2,1)S(1)} async-done(((bf16[64,32,128]{2,1,0:T(8,128)(2,1)}), bf16[64,32,128]{2,1,0:T(8,128)(2,1)S(1)}, u32[]{:S(2)}, u32[]{:S(2)}) %all-to-all-start.1) | async-done | bytes 524320 | tf_op jit(solution)/shard_map/all_to_all | solution.py:330
  71.5 0.7 project.1
  72.3 15.3 %all_to_all.15.sums_ref = bf16[16,32,256]{2,1,0:T(8,128)(2,1)S(1)} all-to-all(bf16[16,32,256]{2,1,0:T(8,128)(2,1)S(1)} %bitcast.10), channel_id=1, replica_groups=mesh['y'=8,'zh'=4,'zp'=2,'tp'=8] {'zp','tp'}, dimensions={0} | all-to-all | bytes 524288 | tf_op jit(solution)/shard_map/all_to_all | solution.py:351
  87.5 0.6 finish.1
  (1 shorter events, 0.0 us)
Async XLA Ops:
  2.3 20.6 %copy-start = (bf16[64,64,128]{2,1,0:T(8,128)(2,1)S(1)}, bf16[64,64,128]{2,1,0:T(8,128)(2,1)}, u32[]{:S(2)}) copy-start(bf16[64,64,128]{2,1,0:T(8,128)(2,1)} %pack_lent.1.packed_ref) | copy-start | bytes 3145732
  2.3 20.6 %copy-start.1 = (bf16[2048,256]{1,0:T(8,128)(2,1)S(1)}, bf16[2048,256]{1,0:T(8,128)(2,1)}, u32[]{:S(2)}) copy-start(bf16[2048,256]{1,0:T(8,128)(2,1)} %mine_ref.1) | copy-start | bytes 3145732
  2.3 42.2 %all-to-all-start = ((bf16[64,64,128]{2,1,0:T(8,128)(2,1)}), bf16[64,64,128]{2,1,0:T(8,128)(2,1)S(1)}, u32[]{:S(2)}, u32[]{:S(2)}) async-start(bf16[64,64,128]{2,1,0:T(8,128)(2,1)} %pack_lent.1.packed_ref), calls=%async_computation | async-start | bytes 2097152 | tf_op jit(solution)/shard_map/all_to_all | solution.py:279
  22.1 0.7 copy-start.11
  22.8 0.7 copy-start.4
  23.6 3.3 %copy-start.2 = (bf16[4,256,1,128]{3,1,2,0:T(8,128)(2,1)S(1)}, bf16[4,256,1,128]{3,1,2,0:T(8,128)(2,1)}, u32[]{:S(2)}) copy-start(bf16[4,256,1,128]{3,1,2,0:T(8,128)(2,1)} %param.15) | copy-start | bytes 786436
  23.6 3.3 %copy-start.3 = (bf16[4,256,1,128]{3,1,2,0:T(8,128)(2,1)S(1)}, bf16[4,256,1,128]{3,1,2,0:T(8,128)(2,1)}, u32[]{:S(2)}) copy-start(bf16[4,256,1,128]{3,1,2,0:T(8,128)(2,1)} %param.16) | copy-start | bytes 786436
  23.6 3.3 %copy-start.5 = (bf16[32,256]{1,0:T(8,128)(2,1)S(1)}, bf16[32,256]{1,0:T(8,128)(2,1)}, u32[]{:S(2)}) copy-start(bf16[32,256]{1,0:T(8,128)(2,1)} %residual_ref.1) | copy-start | bytes 49156
  23.6 3.3 %copy-start.7 = (bf16[4,1,128]{2,0,1:T(4,128)(2,1)S(1)}, bf16[4,1,128]{2,0,1:T(4,128)(2,1)}, u32[]{:S(2)}) copy-start(bf16[4,1,128]{2,0,1:T(4,128)(2,1)} %param.14) | copy-start | bytes 3076
  24.6 35.3 %collective-permute-start = (bf16[1024,256]{1,0:T(8,128)(2,1)}, bf16[1024,256]{1,0:T(8,128)(2,1)S(1)}, u32[]{:S(2)}, u32[]{:S(2)}) collective-permute-start(bf16[1024,256]{1,0:T(8,128)(2,1)} %get-tuple-element.15), channel_id=1, source_target_pairs={{0,8},{8,0},{1,9},{9,1},{2,10},{10,2},{3,11},{11,3},{4,12},{12,4},... | collective-permute-start | bytes 1572872 | tf_op jit(solution)/shard_map/ppermute | solution.py:300
  26.8 0.7 copy-start.6
  26.8 0.7 copy-start.8
  46.3 25.2 %all-to-all-start.1 = ((bf16[64,32,128]{2,1,0:T(8,128)(2,1)}), bf16[64,32,128]{2,1,0:T(8,128)(2,1)S(1)}, u32[]{:S(2)}, u32[]{:S(2)}) async-start(bf16[64,32,128]{2,1,0:T(8,128)(2,1)} %attend.1), calls=%async_computation.1 | async-start | bytes 1048576 | tf_op jit(solution)/shard_map/all_to_all | solution.py:330
  60.0 0.8 copy-start.9
  60.8 1.0 %copy-start.10 = (bf16[1024,256]{1,0:T(8,128)(2,1)S(1)}, bf16[1024,256]{1,0:T(8,128)(2,1)}, u32[]{:S(2)}) copy-start(bf16[1024,256]{1,0:T(8,128)(2,1)} %copy-done.9) | copy-start | bytes 1572868

commit v6 on v5

--- a/solution.py
+++ b/solution.py
@@ -93,15 +93,16 @@
     values_ref[place] = jnp.zeros((32, 128), F32).astype(BF16)
     for load in loads[:3]:
         load.wait()
+    places = [((req_in[63 * here + s] >> 2) - FIRST) & 63 for s in range(63)]
     for s in range(63):
         length = jnp.full((32, 128), len_in[s].astype(F32), F32).astype(BF16)
         keys = jnp.where(token < length, k_in[s], length + ABSENT)
-        keys_ref[((req_in[63 * here + s] >> 2) - FIRST) & 63] = keys
+        keys_ref[places[s]] = keys
     send_keys = pltpu.make_async_copy(keys_ref, out_ref.at[:, pl.ds(0, 32)], sems.at[4])
     send_keys.start()
     loads[3].wait()
     for s in range(63):
-        values_ref[((req_in[63 * here + s] >> 2) - FIRST) & 63] = v_in[s]
+        values_ref[places[s]] = v_in[s]
     send_values = pltpu.make_async_copy(values_ref, out_ref.at[:, pl.ds(32, 32)], sems.at[5])
     send_values.start()
     send_keys.wait()

time: 88.9 us -> 88.9 us (level)
  no operation moved by 1% of the time
where the time goes in v6:
time: 88.9 us; the launch traced here: 88.2 us
  starting transfers between devices  35.6 us (40%)
  waiting for transfers between devices  25.5 us (29%)
  blocking collectives  15.3 us (17%)
  Pallas kernels  7.79 us (9%)
  local copies, waits for them, and re-layouts  3.89 us (4%)
    all_to_all x1, starting transfers between devices, body(): lax.all_to_all(packed, INST, split_axis=0, concat_axis=0, tiled=True, axi...  19.8 us
    all_to_all x1, waiting for transfers between devices, body(): lax.all_to_all(packed, INST, split_axis=0, concat_axis=0, tiled=True, axi...  15.9 us
    all_to_all x1, blocking collectives, body(): lax.all_to_all(partial.reshape(16, 32, 256), ('zp', 'tp'), split_axis=0,...  15.3 us
    all_to_all x1, starting transfers between devices, body(): lax.all_to_all(copies, INST, split_axis=0, concat_axis=0, tiled=True, axi...  13.6 us
    all_to_all x1, waiting for transfers between devices, body(): lax.all_to_all(copies, INST, split_axis=0, concat_axis=0, tiled=True, axi...  9.59 us
    unnamed x24, local copies, waits for them, and re-layouts  3.89 us
    pallas_call x1, Pallas kernels, body(): pl.pallas_call(pack_kernel, out_shape=jax.ShapeDtypeStruct((64, 64, 128),...  2.29 us
    ppermute x1, starting transfers between devices, body(): received = lax.ppermute(sent, 'zp', [(0, 1), (1, 0)])  2.18 us
  transfers between devices with their start and end apart: 3, of which 2 were waited for; matrix products, arithmetic and copies ran while one was open for 0% of the time, Pallas kernels for 5%

profile of v6, /device:TPU:1, one launch (start us, length us, event | category | flops | bytes accessed | tf_op | source)
XLA Modules:
  0.0 88.2 jit_solution(13843754963397090476)
XLA Ops:
  0.0 2.3 %pack_lent.1.packed_ref = bf16[64,64,128]{2,1,0:T(8,128)(2,1)} custom-call(s32[4032]{0:T(1024)} %req_ref.1, s32[63]{0:T(128)} %len_ref.2, bf16[63,32,128]{2,1,0:T(8,128)(2,1)} %bitcast.15, bf16[63,32,128]{2,1,0:T(8,128)(2,1)} %bitcast.16), custom_call_target="tpu_custom_call" | custom-call | tf_op jit(solution)/shard_map/pack_lent/pallas_call | solution.py:259
  2.3 0.0 copy-start
  2.3 0.0 copy-start.1
  2.3 19.8 %all-to-all-start = ((bf16[64,64,128]{2,1,0:T(8,128)(2,1)}), bf16[64,64,128]{2,1,0:T(8,128)(2,1)S(1)}, u32[]{:S(2)}, u32[]{:S(2)}) async-start(bf16[64,64,128]{2,1,0:T(8,128)(2,1)} %pack_lent.1.packed_ref), calls=%async_computation | async-start | bytes 2097152 | tf_op jit(solution)/shard_map/all_to_all | solution.py:280
  22.1 0.0 copy-start.11
  22.2 0.7 copy-done.11
  22.9 0.0 copy-start.4
  22.9 0.0 copy-done
  22.9 0.0 copy-done.1
  22.9 0.7 copy-done.4
  23.6 0.0 copy-start.2
  23.6 0.0 copy-start.3
  23.6 0.0 copy-start.5
  23.6 0.0 copy-start.7
  23.6 1.1 %ask_queries.1 = (bf16[8,128,128]{2,1,0:T(8,128)(2,1)S(1)}, f32[8,128]{1,0:T(8,128)S(1)}, bf16[1024,256]{1,0:T(8,128)(2,1)}) custom-call(s32[1]{0:T(128)} %bitcast.here_ref, s32[32,128]{1,0:T(8,128)S(1)} %pad_bitcast_fusion.table_ref, bf16[4,16,128]{2,1,0:T(8,128)(2,1)S(1)} %copy-done.4, bf16[2048,256]{1,0:T(8,128)(2,1)S(1)} %copy-done.1, ...), custom_call_target="tpu_custom_call" | custom-call | tf_op jit(solution)/shard_map/ask_queries/pallas_call | solution.py:283
  24.7 2.2 %collective-permute-start = (bf16[1024,256]{1,0:T(8,128)(2,1)}, bf16[1024,256]{1,0:T(8,128)(2,1)S(1)}, u32[]{:S(2)}, u32[]{:S(2)}) collective-permute-start(bf16[1024,256]{1,0:T(8,128)(2,1)} %get-tuple-element.15), channel_id=1, source_target_pairs={{0,8},{8,0},{1,9},{9,1},{2,10},{10,2},{3,11},{11,3},{4,12},{12,4},... | collective-permute-start | bytes 1572872 | tf_op jit(solution)/shard_map/ppermute | solution.py:301
  26.9 0.0 copy-start.6
  26.9 0.0 copy-start.8
  26.9 0.0 copy-done.2
  26.9 0.0 copy-done.3
  26.9 0.0 copy-done.5
  26.9 0.0 copy-done.7
  26.9 0.6 copy-done.6
  27.5 0.0 copy-done.8
  27.5 1.1 %home_part.1 = (f32[64,128]{1,0:T(8,128)S(1)}, f32[2,128]{1,0:T(2,128)S(1)}, f32[32,256]{1,0:T(8,128)S(1)}) custom-call(s32[4]{0:T(128)S(1)} %copy-done.8, bf16[4,16,128]{2,1,0:T(8,128)(2,1)S(1)} %copy-done.4, bf16[4,128]{1,0:T(4,128)(2,1)S(1)} %bitcast.13, bf16[4,128]{1,0:T(4,128)(2,1)S(1)} %bitcast.14, bf16[4,256,128]{2,1,0:T(8,128)(2,1)S(1)} %bitcast.11, ...), custom_call_target="tpu_custom_call" | custom-call | tf_op jit(solution)/shard_map/home_part/pallas_call | solution.py:302
  28.6 15.9 %all-to-all-done.recv_ref = bf16[64,64,128]{2,1,0:T(8,128)(2,1)S(1)} async-done(((bf16[64,64,128]{2,1,0:T(8,128)(2,1)}), bf16[64,64,128]{2,1,0:T(8,128)(2,1)S(1)}, u32[]{:S(2)}, u32[]{:S(2)}) %all-to-all-start) | async-done | bytes 1048608 | tf_op jit(solution)/shard_map/all_to_all | solution.py:280
  44.5 1.9 %attend.1 = bf16[64,32,128]{2,1,0:T(8,128)(2,1)} custom-call(bf16[8,128,128]{2,1,0:T(8,128)(2,1)S(1)} %get-tuple-element.11.q_ref, f32[8,128]{1,0:T(8,128)S(1)} %get-tuple-element.12.req_ref, f32[2,128]{1,0:T(2,128)S(1)} %get-tuple-element.13.stat_ref, f32[64,128]{1,0:T(8,128)S(1)} %get-tuple-element.14.home_ref, bf16[64,64,128]{2,1,0:T(8,128)(2,1)S(1)} %all-to-all-done.recv_ref), custom_call_target="tpu_custom_call" | custom-call | tf_op jit(solution)/shard_map/attend/pallas_call | solution.py:322
  46.4 13.6 %all-to-all-start.1 = ((bf16[64,32,128]{2,1,0:T(8,128)(2,1)}), bf16[64,32,128]{2,1,0:T(8,128)(2,1)S(1)}, u32[]{:S(2)}, u32[]{:S(2)}) async-start(bf16[64,32,128]{2,1,0:T(8,128)(2,1)} %attend.1), calls=%async_computation.1 | async-start | bytes 1048576 | tf_op jit(solution)/shard_map/all_to_all | solution.py:331
  60.0 0.0 collective-permute-done.received_ref
  60.0 0.0 copy-start.9
  60.0 0.8 copy-done.9
  60.8 0.0 copy-start.10
  60.8 1.0 %copy-done.10 = bf16[1024,256]{1,0:T(8,128)(2,1)S(1)} copy-done((bf16[1024,256]{1,0:T(8,128)(2,1)S(1)}, bf16[1024,256]{1,0:T(8,128)(2,1)}, u32[]{:S(2)}) %copy-start.10) | copy-done | bytes 524312
  61.8 0.1 join_weights.1.weight_ref
  61.9 9.6 %all-to-all-done.1.rows_ref = bf16[64,32,128]{2,1,0:T(8,128)(2,1)S(1)} async-done(((bf16[64,32,128]{2,1,0:T(8,128)(2,1)}), bf16[64,32,128]{2,1,0:T(8,128)(2,1)S(1)}, u32[]{:S(2)}, u32[]{:S(2)}) %all-to-all-start.1) | async-done | bytes 524320 | tf_op jit(solution)/shard_map/all_to_all | solution.py:331
  71.5 0.7 project.1
  72.3 15.3 %all_to_all.15.sums_ref = bf16[16,32,256]{2,1,0:T(8,128)(2,1)S(1)} all-to-all(bf16[16,32,256]{2,1,0:T(8,128)(2,1)S(1)} %bitcast.10), channel_id=1, replica_groups=mesh['y'=8,'zh'=4,'zp'=2,'tp'=8] {'zp','tp'}, dimensions={0} | all-to-all | bytes 524288 | tf_op jit(solution)/shard_map/all_to_all | solution.py:352
  87.5 0.6 finish.1
  (1 shorter events, 0.0 us)
Async XLA Ops:
  2.3 20.6 %copy-start = (bf16[64,64,128]{2,1,0:T(8,128)(2,1)S(1)}, bf16[64,64,128]{2,1,0:T(8,128)(2,1)}, u32[]{:S(2)}) copy-start(bf16[64,64,128]{2,1,0:T(8,128)(2,1)} %pack_lent.1.packed_ref) | copy-start | bytes 3145732
  2.3 20.6 %copy-start.1 = (bf16[2048,256]{1,0:T(8,128)(2,1)S(1)}, bf16[2048,256]{1,0:T(8,128)(2,1)}, u32[]{:S(2)}) copy-start(bf16[2048,256]{1,0:T(8,128)(2,1)} %mine_ref.1) | copy-start | bytes 3145732
  2.3 42.2 %all-to-all-start = ((bf16[64,64,128]{2,1,0:T(8,128)(2,1)}), bf16[64,64,128]{2,1,0:T(8,128)(2,1)S(1)}, u32[]{:S(2)}, u32[]{:S(2)}) async-start(bf16[64,64,128]{2,1,0:T(8,128)(2,1)} %pack_lent.1.packed_ref), calls=%async_computation | async-start | bytes 2097152 | tf_op jit(solution)/shard_map/all_to_all | solution.py:280
  22.1 0.7 copy-start.11
  22.9 0.7 copy-start.4
  23.6 3.3 %copy-start.2 = (bf16[4,256,1,128]{3,1,2,0:T(8,128)(2,1)S(1)}, bf16[4,256,1,128]{3,1,2,0:T(8,128)(2,1)}, u32[]{:S(2)}) copy-start(bf16[4,256,1,128]{3,1,2,0:T(8,128)(2,1)} %param.15) | copy-start | bytes 786436
  23.6 3.3 %copy-start.3 = (bf16[4,256,1,128]{3,1,2,0:T(8,128)(2,1)S(1)}, bf16[4,256,1,128]{3,1,2,0:T(8,128)(2,1)}, u32[]{:S(2)}) copy-start(bf16[4,256,1,128]{3,1,2,0:T(8,128)(2,1)} %param.16) | copy-start | bytes 786436
  23.6 3.3 %copy-start.5 = (bf16[32,256]{1,0:T(8,128)(2,1)S(1)}, bf16[32,256]{1,0:T(8,128)(2,1)}, u32[]{:S(2)}) copy-start(bf16[32,256]{1,0:T(8,128)(2,1)} %residual_ref.1) | copy-start | bytes 49156
  23.6 3.3 %copy-start.7 = (bf16[4,1,128]{2,0,1:T(4,128)(2,1)S(1)}, bf16[4,1,128]{2,0,1:T(4,128)(2,1)}, u32[]{:S(2)}) copy-start(bf16[4,1,128]{2,0,1:T(4,128)(2,1)} %param.14) | copy-start | bytes 3076
  24.7 35.3 %collective-permute-start = (bf16[1024,256]{1,0:T(8,128)(2,1)}, bf16[1024,256]{1,0:T(8,128)(2,1)S(1)}, u32[]{:S(2)}, u32[]{:S(2)}) collective-permute-start(bf16[1024,256]{1,0:T(8,128)(2,1)} %get-tuple-element.15), channel_id=1, source_target_pairs={{0,8},{8,0},{1,9},{9,1},{2,10},{10,2},{3,11},{11,3},{4,12},{12,4},... | collective-permute-start | bytes 1572872 | tf_op jit(solution)/shard_map/ppermute | solution.py:301
  26.9 0.7 copy-start.6
  26.9 0.7 copy-start.8
  46.4 25.1 %all-to-all-start.1 = ((bf16[64,32,128]{2,1,0:T(8,128)(2,1)}), bf16[64,32,128]{2,1,0:T(8,128)(2,1)S(1)}, u32[]{:S(2)}, u32[]{:S(2)}) async-start(bf16[64,32,128]{2,1,0:T(8,128)(2,1)} %attend.1), calls=%async_computation.1 | async-start | bytes 1048576 | tf_op jit(solution)/shard_map/all_to_all | solution.py:331
  60.0 0.8 copy-start.9
  60.8 1.0 %copy-start.10 = (bf16[1024,256]{1,0:T(8,128)(2,1)S(1)}, bf16[1024,256]{1,0:T(8,128)(2,1)}, u32[]{:S(2)}) copy-start(bf16[1024,256]{1,0:T(8,128)(2,1)} %copy-done.9) | copy-start | bytes 1572868

commit v7 on v6

--- a/solution.py
+++ b/solution.py
@@ -16,7 +16,7 @@
 TN = (((0,), (0,)), ((), ()))
 NN = (((1,), (0,)), ((), ()))
 INST = ("y", "zh", "zp")
-FIRST = 52
+FIRST = 60
 ORDER = [[(FIRST + k) % 64 for k in range(64)]]
 PARAMS = pltpu.CompilerParams(vmem_limit_bytes=16 * 2**20)
 SMEM = pl.BlockSpec(memory_space=pltpu.SMEM)

time: 88.9 us -> 88.4 us (level)
  no operation moved by 1% of the time
where the time goes in v7:
time: 88.4 us; the launch traced here: 87.7 us
  starting transfers between devices  35.3 us (40%)
  waiting for transfers between devices  25.3 us (29%)
  blocking collectives  15.3 us (17%)
  Pallas kernels  7.78 us (9%)
  local copies, waits for them, and re-layouts  3.89 us (4%)
    all_to_all x1, starting transfers between devices, body(): lax.all_to_all(packed, INST, split_axis=0, concat_axis=0, tiled=True, axi...  19.8 us
    all_to_all x1, waiting for transfers between devices, body(): lax.all_to_all(packed, INST, split_axis=0, concat_axis=0, tiled=True, axi...  16 us
    all_to_all x1, blocking collectives, body(): lax.all_to_all(partial.reshape(16, 32, 256), ('zp', 'tp'), split_axis=0,...  15.3 us
    all_to_all x1, starting transfers between devices, body(): lax.all_to_all(copies, INST, split_axis=0, concat_axis=0, tiled=True, axi...  13.3 us
    all_to_all x1, waiting for transfers between devices, body(): lax.all_to_all(copies, INST, split_axis=0, concat_axis=0, tiled=True, axi...  9.31 us
    unnamed x24, local copies, waits for them, and re-layouts  3.89 us
    pallas_call x1, Pallas kernels, body(): pl.pallas_call(pack_kernel, out_shape=jax.ShapeDtypeStruct((64, 64, 128),...  2.29 us
    ppermute x1, starting transfers between devices, body(): received = lax.ppermute(sent, 'zp', [(0, 1), (1, 0)])  2.18 us
  transfers between devices with their start and end apart: 3, of which 2 were waited for; matrix products, arithmetic and copies ran while one was open for 0% of the time, Pallas kernels for 5%

profile of v7, /device:TPU:1, one launch (start us, length us, event | category | flops | bytes accessed | tf_op | source)
XLA Modules:
  0.0 87.7 jit_solution(6100856808240499076)
XLA Ops:
  0.0 2.3 %pack_lent.1.packed_ref = bf16[64,64,128]{2,1,0:T(8,128)(2,1)} custom-call(s32[4032]{0:T(1024)} %req_ref.1, s32[63]{0:T(128)} %len_ref.2, bf16[63,32,128]{2,1,0:T(8,128)(2,1)} %bitcast.15, bf16[63,32,128]{2,1,0:T(8,128)(2,1)} %bitcast.16), custom_call_target="tpu_custom_call" | custom-call | tf_op jit(solution)/shard_map/pack_lent/pallas_call | solution.py:259
  2.3 0.0 copy-start
  2.3 0.0 copy-start.1
  2.3 19.8 %all-to-all-start = ((bf16[64,64,128]{2,1,0:T(8,128)(2,1)}), bf16[64,64,128]{2,1,0:T(8,128)(2,1)S(1)}, u32[]{:S(2)}, u32[]{:S(2)}) async-start(bf16[64,64,128]{2,1,0:T(8,128)(2,1)} %pack_lent.1.packed_ref), calls=%async_computation | async-start | bytes 2097152 | tf_op jit(solution)/shard_map/all_to_all | solution.py:280
  22.1 0.0 copy-start.11
  22.2 0.7 copy-done.11
  22.9 0.0 copy-start.4
  22.9 0.0 copy-done
  22.9 0.0 copy-done.1
  22.9 0.7 copy-done.4
  23.6 0.0 copy-start.2
  23.6 0.0 copy-start.3
  23.6 0.0 copy-start.5
  23.6 0.0 copy-start.7
  23.6 1.1 %ask_queries.1 = (bf16[8,128,128]{2,1,0:T(8,128)(2,1)S(1)}, f32[8,128]{1,0:T(8,128)S(1)}, bf16[1024,256]{1,0:T(8,128)(2,1)}) custom-call(s32[1]{0:T(128)} %bitcast.here_ref, s32[32,128]{1,0:T(8,128)S(1)} %pad_bitcast_fusion.table_ref, bf16[4,16,128]{2,1,0:T(8,128)(2,1)S(1)} %copy-done.4, bf16[2048,256]{1,0:T(8,128)(2,1)S(1)} %copy-done.1, ...), custom_call_target="tpu_custom_call" | custom-call | tf_op jit(solution)/shard_map/ask_queries/pallas_call | solution.py:283
  24.7 2.2 %collective-permute-start = (bf16[1024,256]{1,0:T(8,128)(2,1)}, bf16[1024,256]{1,0:T(8,128)(2,1)S(1)}, u32[]{:S(2)}, u32[]{:S(2)}) collective-permute-start(bf16[1024,256]{1,0:T(8,128)(2,1)} %get-tuple-element.15), channel_id=1, source_target_pairs={{0,8},{8,0},{1,9},{9,1},{2,10},{10,2},{3,11},{11,3},{4,12},{12,4},... | collective-permute-start | bytes 1572872 | tf_op jit(solution)/shard_map/ppermute | solution.py:301
  26.8 0.0 copy-start.6
  26.9 0.0 copy-start.8
  26.9 0.0 copy-done.2
  26.9 0.0 copy-done.3
  26.9 0.0 copy-done.5
  26.9 0.0 copy-done.7
  26.9 0.6 copy-done.6
  27.5 0.0 copy-done.8
  27.5 1.1 %home_part.1 = (f32[64,128]{1,0:T(8,128)S(1)}, f32[2,128]{1,0:T(2,128)S(1)}, f32[32,256]{1,0:T(8,128)S(1)}) custom-call(s32[4]{0:T(128)S(1)} %copy-done.8, bf16[4,16,128]{2,1,0:T(8,128)(2,1)S(1)} %copy-done.4, bf16[4,128]{1,0:T(4,128)(2,1)S(1)} %bitcast.13, bf16[4,128]{1,0:T(4,128)(2,1)S(1)} %bitcast.14, bf16[4,256,128]{2,1,0:T(8,128)(2,1)S(1)} %bitcast.11, ...), custom_call_target="tpu_custom_call" | custom-call | tf_op jit(solution)/shard_map/home_part/pallas_call | solution.py:302
  28.6 16.0 %all-to-all-done.recv_ref = bf16[64,64,128]{2,1,0:T(8,128)(2,1)S(1)} async-done(((bf16[64,64,128]{2,1,0:T(8,128)(2,1)}), bf16[64,64,128]{2,1,0:T(8,128)(2,1)S(1)}, u32[]{:S(2)}, u32[]{:S(2)}) %all-to-all-start) | async-done | bytes 1048608 | tf_op jit(solution)/shard_map/all_to_all | solution.py:280
  44.6 1.9 %attend.1 = bf16[64,32,128]{2,1,0:T(8,128)(2,1)} custom-call(bf16[8,128,128]{2,1,0:T(8,128)(2,1)S(1)} %get-tuple-element.11.q_ref, f32[8,128]{1,0:T(8,128)S(1)} %get-tuple-element.12.req_ref, f32[2,128]{1,0:T(2,128)S(1)} %get-tuple-element.13.stat_ref, f32[64,128]{1,0:T(8,128)S(1)} %get-tuple-element.14.home_ref, bf16[64,64,128]{2,1,0:T(8,128)(2,1)S(1)} %all-to-all-done.recv_ref), custom_call_target="tpu_custom_call" | custom-call | tf_op jit(solution)/shard_map/attend/pallas_call | solution.py:322
  46.5 13.3 %all-to-all-start.1 = ((bf16[64,32,128]{2,1,0:T(8,128)(2,1)}), bf16[64,32,128]{2,1,0:T(8,128)(2,1)S(1)}, u32[]{:S(2)}, u32[]{:S(2)}) async-start(bf16[64,32,128]{2,1,0:T(8,128)(2,1)} %attend.1), calls=%async_computation.1 | async-start | bytes 1048576 | tf_op jit(solution)/shard_map/all_to_all | solution.py:331
  59.8 0.0 collective-permute-done.received_ref
  59.8 0.0 copy-start.9
  59.8 0.8 copy-done.9
  60.6 0.0 copy-start.10
  60.6 1.0 %copy-done.10 = bf16[1024,256]{1,0:T(8,128)(2,1)S(1)} copy-done((bf16[1024,256]{1,0:T(8,128)(2,1)S(1)}, bf16[1024,256]{1,0:T(8,128)(2,1)}, u32[]{:S(2)}) %copy-start.10) | copy-done | bytes 524312
  61.7 0.1 join_weights.1.weight_ref
  61.8 9.3 %all-to-all-done.1.rows_ref = bf16[64,32,128]{2,1,0:T(8,128)(2,1)S(1)} async-done(((bf16[64,32,128]{2,1,0:T(8,128)(2,1)}), bf16[64,32,128]{2,1,0:T(8,128)(2,1)S(1)}, u32[]{:S(2)}, u32[]{:S(2)}) %all-to-all-start.1) | async-done | bytes 524320 | tf_op jit(solution)/shard_map/all_to_all | solution.py:331
  71.1 0.7 project.1
  71.8 15.3 %all_to_all.15.sums_ref = bf16[16,32,256]{2,1,0:T(8,128)(2,1)S(1)} all-to-all(bf16[16,32,256]{2,1,0:T(8,128)(2,1)S(1)} %bitcast.10), channel_id=1, replica_groups=mesh['y'=8,'zh'=4,'zp'=2,'tp'=8] {'zp','tp'}, dimensions={0} | all-to-all | bytes 524288 | tf_op jit(solution)/shard_map/all_to_all | solution.py:352
  87.1 0.6 finish.1
  (1 shorter events, 0.0 us)
Async XLA Ops:
  2.3 20.6 %copy-start = (bf16[64,64,128]{2,1,0:T(8,128)(2,1)S(1)}, bf16[64,64,128]{2,1,0:T(8,128)(2,1)}, u32[]{:S(2)}) copy-start(bf16[64,64,128]{2,1,0:T(8,128)(2,1)} %pack_lent.1.packed_ref) | copy-start | bytes 3145732
  2.3 20.6 %copy-start.1 = (bf16[2048,256]{1,0:T(8,128)(2,1)S(1)}, bf16[2048,256]{1,0:T(8,128)(2,1)}, u32[]{:S(2)}) copy-start(bf16[2048,256]{1,0:T(8,128)(2,1)} %mine_ref.1) | copy-start | bytes 3145732
  2.3 42.2 %all-to-all-start = ((bf16[64,64,128]{2,1,0:T(8,128)(2,1)}), bf16[64,64,128]{2,1,0:T(8,128)(2,1)S(1)}, u32[]{:S(2)}, u32[]{:S(2)}) async-start(bf16[64,64,128]{2,1,0:T(8,128)(2,1)} %pack_lent.1.packed_ref), calls=%async_computation | async-start | bytes 2097152 | tf_op jit(solution)/shard_map/all_to_all | solution.py:280
  22.1 0.7 copy-start.11
  22.9 0.7 copy-start.4
  23.6 3.3 %copy-start.2 = (bf16[4,256,1,128]{3,1,2,0:T(8,128)(2,1)S(1)}, bf16[4,256,1,128]{3,1,2,0:T(8,128)(2,1)}, u32[]{:S(2)}) copy-start(bf16[4,256,1,128]{3,1,2,0:T(8,128)(2,1)} %param.15) | copy-start | bytes 786436
  23.6 3.3 %copy-start.3 = (bf16[4,256,1,128]{3,1,2,0:T(8,128)(2,1)S(1)}, bf16[4,256,1,128]{3,1,2,0:T(8,128)(2,1)}, u32[]{:S(2)}) copy-start(bf16[4,256,1,128]{3,1,2,0:T(8,128)(2,1)} %param.16) | copy-start | bytes 786436
  23.6 3.3 %copy-start.5 = (bf16[32,256]{1,0:T(8,128)(2,1)S(1)}, bf16[32,256]{1,0:T(8,128)(2,1)}, u32[]{:S(2)}) copy-start(bf16[32,256]{1,0:T(8,128)(2,1)} %residual_ref.1) | copy-start | bytes 49156
  23.6 3.3 %copy-start.7 = (bf16[4,1,128]{2,0,1:T(4,128)(2,1)S(1)}, bf16[4,1,128]{2,0,1:T(4,128)(2,1)}, u32[]{:S(2)}) copy-start(bf16[4,1,128]{2,0,1:T(4,128)(2,1)} %param.14) | copy-start | bytes 3076
  24.7 35.2 %collective-permute-start = (bf16[1024,256]{1,0:T(8,128)(2,1)}, bf16[1024,256]{1,0:T(8,128)(2,1)S(1)}, u32[]{:S(2)}, u32[]{:S(2)}) collective-permute-start(bf16[1024,256]{1,0:T(8,128)(2,1)} %get-tuple-element.15), channel_id=1, source_target_pairs={{0,8},{8,0},{1,9},{9,1},{2,10},{10,2},{3,11},{11,3},{4,12},{12,4},... | collective-permute-start | bytes 1572872 | tf_op jit(solution)/shard_map/ppermute | solution.py:301
  26.8 0.7 copy-start.6
  26.9 0.7 copy-start.8
  46.5 24.6 %all-to-all-start.1 = ((bf16[64,32,128]{2,1,0:T(8,128)(2,1)}), bf16[64,32,128]{2,1,0:T(8,128)(2,1)S(1)}, u32[]{:S(2)}, u32[]{:S(2)}) async-start(bf16[64,32,128]{2,1,0:T(8,128)(2,1)} %attend.1), calls=%async_computation.1 | async-start | bytes 1048576 | tf_op jit(solution)/shard_map/all_to_all | solution.py:331
  59.8 0.8 copy-start.9
  60.6 1.0 %copy-start.10 = (bf16[1024,256]{1,0:T(8,128)(2,1)S(1)}, bf16[1024,256]{1,0:T(8,128)(2,1)}, u32[]{:S(2)}) copy-start(bf16[1024,256]{1,0:T(8,128)(2,1)} %copy-done.9) | copy-start | bytes 1572868
